TPU v7x, 32 devices: a whole 2x2x4 slice. The times are simulated.
32 devices in a mesh: face: 4 (over z), elem: 8 (over y, x, core).
Axes of the slice: x: 2, y: 2, z: 4, core: 2. Of those that a mesh axis runs over, the one named last changes fastest.
Arguments:
- tracers: float32 [4, 72, 64, 1024], P(None, None, 'face', 'elem'), may hold values from 0 to 2
- thickness: float32 [72, 64, 1024], P(None, 'face', 'elem'), may hold values from 0.5 to 1.5
- winds: float32 [2, 72, 64, 1024], P(None, None, 'face', 'elem'), may hold values from -4 to 4
- wave_coef: float32 [72], replicated, may hold values from 0.02 to 0.12
- depart: int32 [16, 256], P('face', 'elem'), may hold values from 0 to 4095, as said below
- offsets: int32 [2, 64, 1024], P(None, 'face', 'elem'), may hold values from 0 to 63
Outputs:
- tracer_mass: float32 [4, 72, 64, 1024], P(None, None, 'face', 'elem')
- new_height: float32 [72, 64, 1024], P(None, 'face', 'elem')
- new_winds: float32 [2, 72, 64, 1024], P(None, None, 'face', 'elem')
Inputs may be any that keep to these rules, and one draw needn't show every extreme that they name: depart of element (r, c) is ((r + a) mod 16) * 256 + ((c + b) mod 256) with |a| <= 1 and |b| <= 3; in every device's block of elements both bounds are reached in both directions.
All inputs are finite; a program needn't handle non-finite values.
Results may differ from a plain program's by a relative error of at most 0.0001.
Values sent between devices are 32-bit elements; how exact they have to be, the bound alone decides.
A program may use at most 128 MiB of HBM per device.

v0:
```python
import functools
import math

import jax
import jax.numpy as jnp
import numpy as np
from jax import lax
from jax.experimental import pallas as pl
from jax.experimental.pallas import tpu as pltpu
from jax.sharding import PartitionSpec as P

SUBSTEPS = 2
RX = 3
RY = 1
OFFS = 64


def padded_2(block, sides, width):
    for axis, dim in sides:
        count = lax.axis_size(axis)
        forward = [(i, i + 1) for i in range(count - 1)]
        forward.append((count - 1, 0))
        backward = [(target, source) for source, target in forward]
        low = lax.ppermute(
            lax.slice_in_dim(block, block.shape[dim] - width, None, axis=dim), axis, forward
        )
        high = lax.ppermute(lax.slice_in_dim(block, 0, width, axis=dim), axis, backward)
        block = jnp.concatenate([low, block, high], axis=dim)
    return block


def gll_points():
    inner = 1.0 / math.sqrt(5.0)
    return [-1.0, -inner, inner, 1.0]


def derivative():
    points = gll_points()
    table = np.zeros((4, 4))
    for target in range(4):
        for source in range(4):
            total_value = 0.0
            for other in range(4):
                if other != source:
                    factor = 1.0 / (points[source] - points[other])
                    for fourth in range(4):
                        if fourth != source and fourth != other:
                            factor = (
                                factor
                                * (points[target] - points[fourth])
                                / (points[source] - points[fourth])
                            )
                    total_value = total_value + factor
            table[target, source] = total_value
    return table


def lagrange(coord):
    points = gll_points()
    values_list = []
    for source in range(4):
        value = jnp.ones_like(coord)
        for other in range(4):
            if other != source:
                value = value * ((coord - points[other]) / (points[source] - points[other]))
        values_list.append(value)
    return jnp.stack(values_list, axis=-1)


def along_columns(field):
    count = field.shape[-1] // 4
    matrix = jnp.asarray(np.kron(np.eye(count), derivative().T), jnp.float32)
    return jnp.matmul(field, matrix, precision=lax.Precision.HIGHEST)


def along_rows(field):
    count = field.shape[-2] // 4
    matrix = jnp.asarray(np.kron(np.eye(count), derivative()), jnp.float32)
    return jnp.einsum("ij,...jq->...iq", matrix, field, precision=lax.Precision.HIGHEST)


def edge_average(padded):
    inner_cols = padded.shape[-1] - 2
    column_mod = lax.broadcasted_iota(jnp.int32, (inner_cols,), 0) % 4
    middle = padded[..., 1:-1]
    across = jnp.where(
        column_mod == 3,
        0.5 * (middle + padded[..., 2:]),
        jnp.where(column_mod == 0, 0.5 * (middle + padded[..., :-2]), middle),
    )
    inner_rows = across.shape[-2] - 2
    row_mod = lax.broadcasted_iota(jnp.int32, (inner_rows, 1), 0) % 4
    centre = across[..., 1:-1, :]
    return jnp.where(
        row_mod == 3,
        0.5 * (centre + across[..., 2:, :]),
        jnp.where(row_mod == 0, 0.5 * (centre + across[..., :-2, :]), centre),
    )


def height_rim(field):
    return padded_2(field, (("face", 1), ("elem", 2)), 1)


def wind_rim(field):
    return padded_2(field, (("face", 2), ("elem", 3)), 1)


def wave_substep(height, winds_now, wave_rate, height_pad, wind_pad):
    height = edge_average(
        height_pad(height - wave_rate * (along_columns(winds_now[0]) + along_rows(winds_now[1])))
    )
    pushed = jnp.stack(
        [
            winds_now[0] - wave_rate * along_columns(height),
            winds_now[1] - wave_rate * along_rows(height),
        ]
    )
    return (height, edge_average(wind_pad(pushed)))


def node_weights(offsets):
    coord = -1.0 + (2.0 * offsets.astype(jnp.float32) + 1.0) / OFFS
    across = lagrange(coord[0])
    upward = lagrange(coord[1])
    weights = upward[..., :, None] * across[..., None, :]
    return weights.reshape(offsets.shape[1], offsets.shape[2], 16).transpose(2, 0, 1)


def shift_both(forward_piece, backward_piece, axis):
    count = lax.axis_size(axis)
    forward = [(i, (i + 1) % count) for i in range(count)]
    backward = [(target, source) for source, target in forward]
    return lax.ppermute(forward_piece, axis, forward), lax.ppermute(backward_piece, axis, backward)


def transport_kernel(elem_rows, levels, low, main, high, halo, target, weights, height, out, parts, picked):
    channels = main.shape[1]
    cols = main.shape[2]
    for row in range(4 * (elem_rows + 2)):
        if row < 4:
            middle = low[row]
        elif row < 4 * (elem_rows + 1):
            middle = main[row - 4]
        else:
            middle = high[row - 4 * (elem_rows + 1)]
        whole = jnp.concatenate([middle, halo[row]], axis=1)
        coarse = whole.astype(jnp.bfloat16)
        fine = (whole - coarse.astype(jnp.float32)).astype(jnp.bfloat16)
        at = pl.ds((row % 4) * channels, channels)
        parts[row // 4, 0, at, :] = coarse
        parts[row // 4, 1, at, :] = fine
    width = parts.shape[-1]
    chunk = 24
    for er in range(elem_rows):
        place = lax.broadcasted_iota(jnp.int32, (3 * width, 4 * cols), 0)
        hot = jnp.where(place == target[er : er + 1, :], 1.0, 0.0).astype(jnp.bfloat16)
        for m in range(4):
            at = pl.ds(m * channels, channels)
            total = None
            for piece in range(2):
                left = jnp.concatenate([parts[er + k, piece, at, :] for k in range(3)], axis=1)
                term = jnp.dot(left, hot, preferred_element_type=jnp.float32)
                total = term if total is None else total + term
            picked[m] = total

        @pl.loop(0, channels // chunk)
        def _(step, er=er):
            start = pl.multiple_of(step * chunk, 8)
            level = pl.multiple_of(lax.rem(step, levels // chunk) * chunk, 8)
            nodes = [
                picked[m, pl.ds(start, chunk), n * cols : (n + 1) * cols]
                for m in range(4)
                for n in range(4)
            ]
            lowest = nodes[0]
            highest = nodes[0]
            for node in nodes[1:]:
                lowest = jnp.minimum(lowest, node)
                highest = jnp.maximum(highest, node)
            for a in range(4):
                row = 4 * er + a
                value = weights[0, row : row + 1, :] * nodes[0]
                for s in range(1, 16):
                    value = value + weights[s, row : row + 1, :] * nodes[s]
                value = jnp.minimum(jnp.maximum(value, lowest), highest)
                out[pl.ds(start, chunk), row, :] = value * height[row, pl.ds(level, chunk), :]


def transport(tracers, height, depart, offsets):
    count, levels, node_rows, node_cols = tracers.shape
    elem_rows = node_rows // 4
    elem_cols = node_cols // 4
    channels = count * levels
    face_at = lax.axis_index("face")
    elem_at = lax.axis_index("elem")
    grid_rows = elem_rows * lax.axis_size("face")
    grid_cols = elem_cols * lax.axis_size("elem")
    rows_first = tracers.reshape(channels, node_rows, node_cols).transpose(1, 0, 2)
    low, high = shift_both(rows_first[-4:], rows_first[:4], "face")
    edge = 4 * RX
    left, right = shift_both(
        rows_first[:, :, -edge:].transpose(0, 2, 1), rows_first[:, :, :edge].transpose(0, 2, 1), "elem"
    )
    sides = jnp.concatenate([left, right], axis=1)
    under, above = shift_both(sides[-4:], sides[:4], "face")
    sides = jnp.concatenate([under, sides, above], axis=0)
    halo = jnp.pad(sides, ((0, 0), (0, node_cols - 2 * edge), (0, 0))).transpose(0, 2, 1)

    row_index = lax.broadcasted_iota(jnp.int32, (elem_rows, elem_cols), 0)
    col_index = lax.broadcasted_iota(jnp.int32, (elem_rows, elem_cols), 1)
    source_row = depart // grid_cols
    source_col = depart % grid_cols
    row_shift = (source_row - (face_at * elem_rows + row_index) + RY) % grid_rows
    col_shift = (source_col - (elem_at * elem_cols + col_index) + RX) % grid_cols - RX
    first = jnp.repeat(4 * (col_index + col_shift), 4, axis=1)
    which = jnp.repeat(row_shift, 4, axis=1)
    width = 2 * node_cols
    targets = []
    for n in range(4):
        col = first + n
        spot = jnp.where(col < 0, node_cols + edge + col, jnp.where(col < node_cols, col, col + edge))
        targets.append(which * width + spot)
    target = jnp.concatenate(targets, axis=1)
    weights = node_weights(offsets)
    out = pl.pallas_call(
        functools.partial(transport_kernel, elem_rows, levels),
        out_shape=jax.ShapeDtypeStruct((channels, node_rows, node_cols), jnp.float32),
        in_specs=[pl.BlockSpec(memory_space=pltpu.VMEM)] * 7,
        out_specs=pl.BlockSpec(memory_space=pltpu.VMEM),
        scratch_shapes=[
            pltpu.VMEM((elem_rows + 2, 2, 4 * channels, width), jnp.bfloat16),
            pltpu.VMEM((4, channels, 4 * node_cols), jnp.float32),
        ],
        compiler_params=pltpu.CompilerParams(vmem_limit_bytes=48 * 1024 * 1024),
        name="transport",
    )(low, rows_first, high, halo, target, weights, height.transpose(1, 0, 2))
    return out.reshape(tracers.shape)


def body(tracers, thickness, winds, wave_coef, depart, offsets):
    wave_rate = wave_coef[:, None, None]
    height = thickness
    winds_now = winds
    for substep in range(SUBSTEPS):
        height, winds_now = wave_substep(height, winds_now, wave_rate, height_rim, wind_rim)
    return (transport(tracers, height, depart, offsets), height, winds_now)


def solution(mesh):
    in_specs = (
        P(None, None, "face", "elem"),
        P(None, "face", "elem"),
        P(None, None, "face", "elem"),
        P(),
        P("face", "elem"),
        P(None, "face", "elem"),
    )
    out_specs = (
        P(None, None, "face", "elem"),
        P(None, "face", "elem"),
        P(None, None, "face", "elem"),
    )
    return jax.shard_map(body, mesh=mesh, in_specs=in_specs, out_specs=out_specs, check_vma=False)
```

profile of v0, /device:TPU:0, one launch (start us, length us, event | category | flops | bytes accessed | tf_op | source)
XLA Modules:
  0.0 170.2 jit_solution(478824432999928300)
XLA Ops:
  0.7 2.3 %fusion.81 = (f32[1,72,16,128]{3,2,1,0:T(8,128)}, f32[1,72,16,128]{3,2,1,0:T(8,128)S(1)}) fusion(f32[2,72,16,128]{3,2,1,0:T(8,128)} %param.16), kind=kLoop, calls=%fused_computation.180 | loop fusion | bytes 2359296 | tf_op jit(solution)/shard_map/slice | solution.py:111
  5.3 3.0 %collective-permute-start.6 = (f32[72,1,128]{2,0,1:T(8,128)}, f32[72,1,128]{2,0,1:T(8,128)}, u32[]{:S(2)}, u32[]{:S(2)}) collective-permute-start(f32[72,1,128]{2,0,1:T(8,128)} %get-tuple-element.34), channel_id=1, source_target_pairs={{0,8},{8,16},{16,24},{24,0},{1,9},{9,17},{17,25},{25,1},{2,10},{10... | collective-permute-start | bytes 110600 | tf_op jit(solution)/shard_map/ppermute | solution.py:24
  8.4 2.0 %collective-permute-start.7 = (f32[72,1,128]{2,0,1:T(8,128)}, f32[72,1,128]{2,0,1:T(8,128)}, u32[]{:S(2)}, u32[]{:S(2)}) collective-permute-start(f32[72,1,128]{2,0,1:T(8,128)} %get-tuple-element.35), channel_id=1, source_target_pairs={{8,0},{16,8},{24,16},{0,24},{9,1},{17,9},{25,17},{1,25},{10,2},{18... | collective-permute-start | bytes 110600 | tf_op jit(solution)/shard_map/ppermute | solution.py:27
  11.2 3.0 %slice_bitcast_fusion.1 = (f32[16,12,288]{1,2,0:T(8,128)}, f32[16,12,288]{1,2,0:T(8,128)}) fusion(f32[16,288,128]{2,1,0:T(8,128)S(1)} %bitcast.93), kind=kLoop, calls=%fused_computation.2 | loop fusion | bytes 884736 | tf_op jit(solution)/shard_map/transpose | solution.py:203
  14.1 3.3 %copy.58 = f32[16,12,288]{2,0,1:T(8,128)} copy(f32[16,12,288]{1,2,0:T(8,128)} %get-tuple-element.12) | data formatting | bytes 442368 | tf_op jit(solution)/shard_map/transpose | solution.py:203
  17.4 3.3 %copy.59 = f32[16,12,288]{2,0,1:T(8,128)} copy(f32[16,12,288]{1,2,0:T(8,128)} %get-tuple-element.13) | data formatting | bytes 442368 | tf_op jit(solution)/shard_map/transpose | solution.py:203
  20.7 2.6 %collective-permute-start.3 = (f32[16,12,288]{2,0,1:T(8,128)}, f32[16,12,288]{2,0,1:T(8,128)}, u32[]{:S(2)}, u32[]{:S(2)}) collective-permute-start(f32[16,12,288]{2,0,1:T(8,128)} %copy.59), channel_id=1, source_target_pairs={{1,0},{2,1},{3,2},{4,3},{5,4},{6,5},{7,6},{0,7},{9,8},{10,9},{11,1... | collective-permute-start | bytes 663560 | tf_op jit(solution)/shard_map/ppermute | solution.py:134
  28.6 1.9 %copy.68 = f32[72,18,1]{0,2,1:T(1,128)} copy(f32[72,18,1]{2,0,1:T(8,128)} %get-tuple-element.30) | data formatting | bytes 10368 | tf_op jit(solution)/shard_map/slice | solution.py:27
  30.7 1.9 %copy.70 = f32[72,18,1]{0,2,1:T(1,128)} copy(f32[72,18,1]{2,0,1:T(8,128)} %get-tuple-element.31) | data formatting | bytes 10368 | tf_op jit(solution)/shard_map/slice | solution.py:25
  38.7 1.9 %fusion.38 = f32[72,18,128]{2,0,1:T(8,128)S(1)} fusion(f32[72,18,1]{2,0,1:T(8,128)} %copy.71, f32[72,1,128]{2,0,1:T(8,128)} %collective-permute-done.7, f32[72,16,128]{2,0,1:T(8,128)S(1)} %fusion.20, f32[72,1,128]{2,0,1:T(8,128)} %collective-permute-done.6, f32[72,18,1]{2,0,1:T(8,128)} %copy.69, pred[128]{0:T(512)(128)(4,1)S(1)} %copy-done.40, ...), kind=kLoop, calls=%fused_computation.75 | loop fusion | flops 2322432 | bytes 1337728 | tf_op jit(solution)/shard_map/jit(_where)/select_n | solution.py:86
  45.0 2.4 %collective-permute-start.11 = (f32[2,72,1,128]{3,1,2,0:T(8,128)S(1)}, f32[2,72,1,128]{3,1,2,0:T(8,128)S(1)}, u32[]{:S(2)}, u32[]{:S(2)}) collective-permute-start(f32[2,72,1,128]{3,1,2,0:T(8,128)S(1)} %get-tuple-element.23), channel_id=1, source_target_pairs={{8,0},{16,8},{24,16},{0,24},{9,1},{17,9},{25,17},{1,25},{10,2},{18... | collective-permute-start | bytes 221192 | tf_op jit(solution)/shard_map/ppermute | solution.py:27
  47.9 2.3 %collective-permute-done.10 = f32[2,72,1,128]{3,1,2,0:T(8,128)S(1)} collective-permute-done((f32[2,72,1,128]{3,1,2,0:T(8,128)S(1)}, f32[2,72,1,128]{3,1,2,0:T(8,128)S(1)}, u32[]{:S(2)}, u32[]{:S(2)}) %collective-permute-start.10) | collective-permute-done | bytes 73760 | tf_op jit(solution)/shard_map/ppermute | solution.py:24
  53.6 2.4 %copy.76 = f32[2,72,18,1]{1,0,3,2:T(2,128)} copy(f32[2,72,18,1]{3,1,2,0:T(8,128)} %get-tuple-element.18) | data formatting | bytes 20736 | tf_op jit(solution)/shard_map/slice | solution.py:27
  55.9 2.4 %copy.78 = f32[2,72,18,1]{1,0,3,2:T(2,128)} copy(f32[2,72,18,1]{3,1,2,0:T(8,128)} %get-tuple-element.19) | data formatting | bytes 20736 | tf_op jit(solution)/shard_map/slice | solution.py:25
  65.1 2.3 %copy.77 = f32[2,72,18,1]{3,1,2,0:T(8,128)} copy(f32[2,72,18,1]{1,0,3,2:T(2,128)} %collective-permute-done.12) | data formatting | bytes 20736 | tf_op jit(solution)/shard_map/ppermute | solution.py:27
  67.3 2.3 %copy.79 = f32[2,72,18,1]{3,1,2,0:T(8,128)} copy(f32[2,72,18,1]{1,0,3,2:T(2,128)} %collective-permute-done.13) | data formatting | bytes 20736 | tf_op jit(solution)/shard_map/ppermute | solution.py:24
  69.6 4.2 %fusion.9 = f32[2,72,18,128]{3,1,2,0:T(8,128)S(1)} fusion(f32[2,72,18,1]{3,1,2,0:T(8,128)} %copy.79, f32[2,72,1,128]{3,1,2,0:T(8,128)} %copy-done.25, f32[2,72,1,128]{3,1,2,0:T(8,128)} %copy-done.24, f32[1,72,16,128]{3,1,2,0:T(8,128)} %copy-done.6, f32[1,72,16,128]{3,1,2,0:T(8,128)} %copy-done.5, f32[2,72,18,1]{3,1,2,0:T(8,128)} %copy.77, ...), kind=kLoop, calls=%fused_computation.21 | loop fusion | flops 5640192 | bytes 2675200 | tf_op jit(solution)/shard_map/jit(_where)/select_n | solution.py:86
  77.5 2.6 %collective-permute-start.15 = (f32[72,1,128]{2,0,1:T(8,128)S(1)}, f32[72,1,128]{2,0,1:T(8,128)S(1)}, u32[]{:S(2)}, u32[]{:S(2)}) collective-permute-start(f32[72,1,128]{2,0,1:T(8,128)S(1)} %get-tuple-element.33), channel_id=1, source_target_pairs={{8,0},{16,8},{24,16},{0,24},{9,1},{17,9},{25,17},{1,25},{10,2},{18... | collective-permute-start | bytes 110600 | tf_op jit(solution)/shard_map/ppermute | solution.py:27
  84.6 2.0 %copy.84 = f32[72,18,1]{0,2,1:T(1,128)} copy(f32[72,18,1]{2,0,1:T(8,128)} %get-tuple-element.28) | data formatting | bytes 10368 | tf_op jit(solution)/shard_map/slice | solution.py:27
  87.8 1.9 %copy.86 = f32[72,18,1]{0,2,1:T(1,128)} copy(f32[72,18,1]{2,0,1:T(8,128)} %get-tuple-element.29) | data formatting | bytes 10368 | tf_op jit(solution)/shard_map/slice | solution.py:25
  95.8 2.0 %fusion.32 = f32[72,18,128]{2,0,1:T(8,128)S(1)} fusion(f32[72,18,1]{2,0,1:T(8,128)} %copy.87, f32[72,1,128]{2,0,1:T(8,128)} %copy-done.27, f32[72,16,128]{2,0,1:T(8,128)S(1)} %copy-done.8, f32[72,1,128]{2,0,1:T(8,128)} %copy-done.26, f32[72,18,1]{2,0,1:T(8,128)} %copy.85, pred[128]{0:T(512)(128)(4,1)} %get-tuple-element.52, pred[128]{0:T(512)(128)(4,1)} %get-tuple-element.53), kind=kLoop, calls=%fused_computation.63 | loop fusion | flops 2322432 | bytes 1337728 | tf_op jit(solution)/shard_map/jit(_where)/select_n | solution.py:86
  100.8 3.8 %collective-permute-start.19 = (f32[2,72,1,128]{3,1,2,0:T(8,128)S(1)}, f32[2,72,1,128]{3,1,2,0:T(8,128)S(1)}, u32[]{:S(2)}, u32[]{:S(2)}) collective-permute-start(f32[2,72,1,128]{3,1,2,0:T(8,128)S(1)} %get-tuple-element.21), channel_id=1, source_target_pairs={{8,0},{16,8},{24,16},{0,24},{9,1},{17,9},{25,17},{1,25},{10,2},{18... | collective-permute-start | bytes 221192 | tf_op jit(solution)/shard_map/ppermute | solution.py:27
  112.8 2.4 %copy.92 = f32[2,72,18,1]{1,0,3,2:T(2,128)} copy(f32[2,72,18,1]{3,1,2,0:T(8,128)} %get-tuple-element.16) | data formatting | bytes 20736 | tf_op jit(solution)/shard_map/slice | solution.py:27
  115.2 2.4 %copy.94 = f32[2,72,18,1]{1,0,3,2:T(2,128)} copy(f32[2,72,18,1]{3,1,2,0:T(8,128)} %get-tuple-element.17) | data formatting | bytes 20736 | tf_op jit(solution)/shard_map/slice | solution.py:25
  120.9 11.4 %collective-permute-start.5 = (f32[4,24,288]{2,1,0:T(8,128)}, f32[4,24,288]{2,1,0:T(8,128)}, u32[]{:S(2)}, u32[]{:S(2)}) collective-permute-start(f32[4,24,288]{2,1,0:T(8,128)} %get-tuple-element.27), channel_id=1, source_target_pairs={{8,0},{16,8},{24,16},{0,24},{9,1},{17,9},{25,17},{1,25},{10,2},{18... | collective-permute-start | bytes 331784 | tf_op jit(solution)/shard_map/ppermute | solution.py:134
  132.3 2.3 %copy.93 = f32[2,72,18,1]{3,1,2,0:T(8,128)} copy(f32[2,72,18,1]{1,0,3,2:T(2,128)} %collective-permute-done.20) | data formatting | bytes 20736 | tf_op jit(solution)/shard_map/ppermute | solution.py:27
  134.6 2.3 %copy.95 = f32[2,72,18,1]{3,1,2,0:T(8,128)} copy(f32[2,72,18,1]{1,0,3,2:T(2,128)} %collective-permute-done.21) | data formatting | bytes 20736 | tf_op jit(solution)/shard_map/ppermute | solution.py:24
  136.9 4.2 %fusion.3 = f32[2,72,18,128]{3,1,2,0:T(8,128)S(1)} fusion(f32[2,72,18,1]{3,1,2,0:T(8,128)} %copy.95, f32[2,72,1,128]{3,1,2,0:T(8,128)} %copy-done.23, f32[2,72,1,128]{3,1,2,0:T(8,128)} %copy-done.22, f32[1,72,16,128]{3,1,2,0:T(8,128)} %copy-done.4, f32[1,72,16,128]{3,1,2,0:T(8,128)} %copy-done.3, f32[2,72,18,1]{3,1,2,0:T(8,128)} %copy.93, ...), kind=kLoop, calls=%fused_computation.7 | loop fusion | flops 5640192 | bytes 2675200 | tf_op jit(solution)/shard_map/jit(_where)/select_n | solution.py:86
  143.0 2.0 %pad_maximum_fusion.18 = f32[24,24,288]{2,1,0:T(8,128)} fusion(f32[4,24,288]{2,1,0:T(8,128)} %collective-permute-done.5, f32[16,12,288]{2,1,0:T(8,128)S(1)} %copy-done.12, f32[16,12,288]{2,1,0:T(8,128)S(1)} %copy-done.11, f32[4,24,288]{2,1,0:T(8,128)} %collective-permute-done.4), kind=kLoop, calls=%fused_computation.58 | loop fusion | flops 497664 | bytes 1327104 | tf_op jit(solution)/shard_map/concatenate | solution.py:207
  145.0 3.3 %copy.62 = f32[24,24,288]{1,2,0:T(8,128)} copy(f32[24,24,288]{2,1,0:T(8,128)} %pad_maximum_fusion.18) | data formatting | bytes 1327104 | tf_op jit(solution)/shard_map/concatenate | solution.py:207
  148.3 4.1 %pad_bitcast_fusion.halo = f32[24,288,128]{2,1,0:T(8,128)} fusion(f32[24,24,288]{1,2,0:T(8,128)} %copy.62), kind=kLoop, calls=%fused_computation | loop fusion | bytes 4202496 | tf_op jit(solution)/shard_map/transpose | solution.py:208
  152.4 17.8 %transport.1 = f32[288,16,128]{2,1,0:T(8,128)} custom-call(f32[4,288,128]{2,1,0:T(8,128)S(1)} %collective-permute-done.low, f32[16,288,128]{2,1,0:T(8,128)S(1)} %bitcast.95, f32[4,288,128]{2,1,0:T(8,128)} %collective-permute-done.1.high, f32[24,288,128]{2,1,0:T(8,128)} %pad_bitcast_fusion.halo, s32[4,512]{1,0:T(4,128)S(1)} %pad_add_fusion.target, ...), custom_call_target="tpu_custom_call" | custom-call | tf_op jit(solution)/shard_map/transport/pallas_call | solution.py:226
  (180 shorter events, 61.0 us)
Async XLA Ops:
  3.6 6.8 %copy-start.14 = (f32[4,72,16,128]{3,2,1,0:T(8,128)S(1)}, f32[4,72,16,128]{3,2,1,0:T(8,128)}, u32[]{:S(2)}) copy-start(f32[4,72,16,128]{3,2,1,0:T(8,128)} %param.14) | copy-start | bytes 7077892
  5.3 21.2 %collective-permute-start.6 = (f32[72,1,128]{2,0,1:T(8,128)}, f32[72,1,128]{2,0,1:T(8,128)}, u32[]{:S(2)}, u32[]{:S(2)}) collective-permute-start(f32[72,1,128]{2,0,1:T(8,128)} %get-tuple-element.34), channel_id=1, source_target_pairs={{0,8},{8,16},{16,24},{24,0},{1,9},{9,17},{17,25},{25,1},{2,10},{10... | collective-permute-start | bytes 110600 | tf_op jit(solution)/shard_map/ppermute | solution.py:24
  8.4 18.1 %collective-permute-start.7 = (f32[72,1,128]{2,0,1:T(8,128)}, f32[72,1,128]{2,0,1:T(8,128)}, u32[]{:S(2)}, u32[]{:S(2)}) collective-permute-start(f32[72,1,128]{2,0,1:T(8,128)} %get-tuple-element.35), channel_id=1, source_target_pairs={{8,0},{16,8},{24,16},{0,24},{9,1},{17,9},{25,17},{1,25},{10,2},{18... | collective-permute-start | bytes 110600 | tf_op jit(solution)/shard_map/ppermute | solution.py:27
  17.4 87.5 %collective-permute-start.2 = (f32[16,12,288]{2,0,1:T(8,128)}, f32[16,12,288]{2,0,1:T(8,128)}, u32[]{:S(2)}, u32[]{:S(2)}) collective-permute-start(f32[16,12,288]{2,0,1:T(8,128)} %copy.58), channel_id=1, source_target_pairs={{0,1},{1,2},{2,3},{3,4},{4,5},{5,6},{6,7},{7,0},{8,9},{9,10},{10,1... | collective-permute-start | bytes 663560 | tf_op jit(solution)/shard_map/ppermute | solution.py:134
  20.7 87.0 %collective-permute-start.3 = (f32[16,12,288]{2,0,1:T(8,128)}, f32[16,12,288]{2,0,1:T(8,128)}, u32[]{:S(2)}, u32[]{:S(2)}) collective-permute-start(f32[16,12,288]{2,0,1:T(8,128)} %copy.59), channel_id=1, source_target_pairs={{1,0},{2,1},{3,2},{4,3},{5,4},{6,5},{7,6},{0,7},{9,8},{10,9},{11,1... | collective-permute-start | bytes 663560 | tf_op jit(solution)/shard_map/ppermute | solution.py:134
  24.6 127.8 %collective-permute-start = (f32[4,288,128]{2,1,0:T(8,128)}, f32[4,288,128]{2,1,0:T(8,128)S(1)}, u32[]{:S(2)}, u32[]{:S(2)}) collective-permute-start(f32[4,288,128]{2,1,0:T(8,128)} %get-tuple-element.15), channel_id=1, source_target_pairs={{0,8},{8,16},{16,24},{24,0},{1,9},{9,17},{17,25},{25,1},{2,10},{10... | collective-permute-start | bytes 1769480 | tf_op jit(solution)/shard_map/ppermute | solution.py:134
  26.5 47.4 %copy-start.33 = (pred[16]{0:T(512)(128)(4,1)}, pred[16]{0:T(512)(128)(4,1)S(1)}, u32[]{:S(2)}) copy-start(pred[16]{0:T(512)(128)(4,1)S(1)} %get-tuple-element.54) | copy-start | bytes 52
  28.6 10.1 %copy-start.40 = (pred[128]{0:T(512)(128)(4,1)S(1)}, pred[128]{0:T(512)(128)(4,1)}, u32[]{:S(2)}) copy-start(pred[128]{0:T(512)(128)(4,1)} %get-tuple-element.52) | copy-start | bytes 388
  30.5 3.0 %collective-permute-start.8 = (f32[72,18,1]{0,2,1:T(1,128)}, f32[72,18,1]{0,2,1:T(1,128)}, u32[]{:S(2)}, u32[]{:S(2)}) collective-permute-start(f32[72,18,1]{0,2,1:T(1,128)} %copy.68), channel_id=1, source_target_pairs={{1,0},{2,1},{3,2},{4,3},{5,4},{6,5},{7,6},{0,7},{9,8},{10,9},{11,1... | collective-permute-start | bytes 15560 | tf_op jit(solution)/shard_map/ppermute | solution.py:27
  32.6 4.3 %collective-permute-start.9 = (f32[72,18,1]{0,2,1:T(1,128)}, f32[72,18,1]{0,2,1:T(1,128)}, u32[]{:S(2)}, u32[]{:S(2)}) collective-permute-start(f32[72,18,1]{0,2,1:T(1,128)} %copy.70), channel_id=1, source_target_pairs={{0,1},{1,2},{2,3},{3,4},{4,5},{5,6},{6,7},{7,0},{8,9},{9,10},{10,1... | collective-permute-start | bytes 15560 | tf_op jit(solution)/shard_map/ppermute | solution.py:24
  42.5 7.8 %copy-start.5 = (f32[1,72,16,128]{3,1,2,0:T(8,128)}, f32[1,72,16,128]{3,1,2,0:T(8,128)S(1)}, u32[]{:S(2)}) copy-start(f32[1,72,16,128]{3,1,2,0:T(8,128)S(1)} %fusion.17) | copy-start | bytes 1769476
  43.5 6.8 %copy-start.6 = (f32[1,72,16,128]{3,1,2,0:T(8,128)}, f32[1,72,16,128]{3,1,2,0:T(8,128)S(1)}, u32[]{:S(2)}) copy-start(f32[1,72,16,128]{3,1,2,0:T(8,128)S(1)} %fusion.52) | copy-start | bytes 1769476
  43.5 6.7 %collective-permute-start.10 = (f32[2,72,1,128]{3,1,2,0:T(8,128)S(1)}, f32[2,72,1,128]{3,1,2,0:T(8,128)S(1)}, u32[]{:S(2)}, u32[]{:S(2)}) collective-permute-start(f32[2,72,1,128]{3,1,2,0:T(8,128)S(1)} %get-tuple-element.22), channel_id=1, source_target_pairs={{0,8},{8,16},{16,24},{24,0},{1,9},{9,17},{17,25},{25,1},{2,10},{10... | collective-permute-start | bytes 221192 | tf_op jit(solution)/shard_map/ppermute | solution.py:24
  45.0 5.3 %collective-permute-start.11 = (f32[2,72,1,128]{3,1,2,0:T(8,128)S(1)}, f32[2,72,1,128]{3,1,2,0:T(8,128)S(1)}, u32[]{:S(2)}, u32[]{:S(2)}) collective-permute-start(f32[2,72,1,128]{3,1,2,0:T(8,128)S(1)} %get-tuple-element.23), channel_id=1, source_target_pairs={{8,0},{16,8},{24,16},{0,24},{9,1},{17,9},{25,17},{1,25},{10,2},{18... | collective-permute-start | bytes 221192 | tf_op jit(solution)/shard_map/ppermute | solution.py:27
  55.9 9.1 %collective-permute-start.12 = (f32[2,72,18,1]{1,0,3,2:T(2,128)}, f32[2,72,18,1]{1,0,3,2:T(2,128)}, u32[]{:S(2)}, u32[]{:S(2)}) collective-permute-start(f32[2,72,18,1]{1,0,3,2:T(2,128)} %copy.76), channel_id=1, source_target_pairs={{1,0},{2,1},{3,2},{4,3},{5,4},{6,5},{7,6},{0,7},{9,8},{10,9},{11,1... | collective-permute-start | bytes 31112 | tf_op jit(solution)/shard_map/ppermute | solution.py:27
  58.3 9.0 %collective-permute-start.13 = (f32[2,72,18,1]{1,0,3,2:T(2,128)}, f32[2,72,18,1]{1,0,3,2:T(2,128)}, u32[]{:S(2)}, u32[]{:S(2)}) collective-permute-start(f32[2,72,18,1]{1,0,3,2:T(2,128)} %copy.78), channel_id=1, source_target_pairs={{0,1},{1,2},{2,3},{3,4},{4,5},{5,6},{6,7},{7,0},{8,9},{9,10},{10,1... | collective-permute-start | bytes 31112 | tf_op jit(solution)/shard_map/ppermute | solution.py:24
  76.2 5.8 %collective-permute-start.14 = (f32[72,1,128]{2,0,1:T(8,128)S(1)}, f32[72,1,128]{2,0,1:T(8,128)S(1)}, u32[]{:S(2)}, u32[]{:S(2)}) collective-permute-start(f32[72,1,128]{2,0,1:T(8,128)S(1)} %get-tuple-element.32), channel_id=1, source_target_pairs={{0,8},{8,16},{16,24},{24,0},{1,9},{9,17},{17,25},{25,1},{2,10},{10... | collective-permute-start | bytes 110600 | tf_op jit(solution)/shard_map/ppermute | solution.py:24
  77.5 4.6 %collective-permute-start.15 = (f32[72,1,128]{2,0,1:T(8,128)S(1)}, f32[72,1,128]{2,0,1:T(8,128)S(1)}, u32[]{:S(2)}, u32[]{:S(2)}) collective-permute-start(f32[72,1,128]{2,0,1:T(8,128)S(1)} %get-tuple-element.33), channel_id=1, source_target_pairs={{8,0},{16,8},{24,16},{0,24},{9,1},{17,9},{25,17},{1,25},{10,2},{18... | collective-permute-start | bytes 110600 | tf_op jit(solution)/shard_map/ppermute | solution.py:27
  84.6 11.3 %copy-start.8 = (f32[72,16,128]{2,0,1:T(8,128)S(1)}, f32[72,16,128]{2,0,1:T(8,128)}, u32[]{:S(2)}) copy-start(f32[72,16,128]{2,0,1:T(8,128)} %copy-done.7) | copy-start | bytes 1769476
  86.6 3.8 %collective-permute-start.16 = (f32[72,18,1]{0,2,1:T(1,128)}, f32[72,18,1]{0,2,1:T(1,128)}, u32[]{:S(2)}, u32[]{:S(2)}) collective-permute-start(f32[72,18,1]{0,2,1:T(1,128)} %copy.84), channel_id=1, source_target_pairs={{1,0},{2,1},{3,2},{4,3},{5,4},{6,5},{7,6},{0,7},{9,8},{10,9},{11,1... | collective-permute-start | bytes 15560 | tf_op jit(solution)/shard_map/ppermute | solution.py:27
  89.7 4.3 %collective-permute-start.17 = (f32[72,18,1]{0,2,1:T(1,128)}, f32[72,18,1]{0,2,1:T(1,128)}, u32[]{:S(2)}, u32[]{:S(2)}) collective-permute-start(f32[72,18,1]{0,2,1:T(1,128)} %copy.86), channel_id=1, source_target_pairs={{0,1},{1,2},{2,3},{3,4},{4,5},{5,6},{6,7},{7,0},{8,9},{9,10},{10,1... | collective-permute-start | bytes 15560 | tf_op jit(solution)/shard_map/ppermute | solution.py:24
  99.7 9.8 %copy-start.3 = (f32[1,72,16,128]{3,1,2,0:T(8,128)}, f32[1,72,16,128]{3,1,2,0:T(8,128)S(1)}, u32[]{:S(2)}) copy-start(f32[1,72,16,128]{3,1,2,0:T(8,128)S(1)} %fusion.13) | copy-start | bytes 1769476
  100.7 8.8 %copy-start.4 = (f32[1,72,16,128]{3,1,2,0:T(8,128)}, f32[1,72,16,128]{3,1,2,0:T(8,128)S(1)}, u32[]{:S(2)}) copy-start(f32[1,72,16,128]{3,1,2,0:T(8,128)S(1)} %fusion.53) | copy-start | bytes 1769476
  100.8 8.8 %collective-permute-start.18 = (f32[2,72,1,128]{3,1,2,0:T(8,128)S(1)}, f32[2,72,1,128]{3,1,2,0:T(8,128)S(1)}, u32[]{:S(2)}, u32[]{:S(2)}) collective-permute-start(f32[2,72,1,128]{3,1,2,0:T(8,128)S(1)} %get-tuple-element.20), channel_id=1, source_target_pairs={{0,8},{8,16},{16,24},{24,0},{1,9},{9,17},{17,25},{25,1},{2,10},{10... | collective-permute-start | bytes 221192 | tf_op jit(solution)/shard_map/ppermute | solution.py:24
  100.8 8.7 %collective-permute-start.19 = (f32[2,72,1,128]{3,1,2,0:T(8,128)S(1)}, f32[2,72,1,128]{3,1,2,0:T(8,128)S(1)}, u32[]{:S(2)}, u32[]{:S(2)}) collective-permute-start(f32[2,72,1,128]{3,1,2,0:T(8,128)S(1)} %get-tuple-element.21), channel_id=1, source_target_pairs={{8,0},{16,8},{24,16},{0,24},{9,1},{17,9},{25,17},{1,25},{10,2},{18... | collective-permute-start | bytes 221192 | tf_op jit(solution)/shard_map/ppermute | solution.py:27
  104.9 47.5 %collective-permute-start.1 = (f32[4,288,128]{2,1,0:T(8,128)}, f32[4,288,128]{2,1,0:T(8,128)}, u32[]{:S(2)}, u32[]{:S(2)}) collective-permute-start(f32[4,288,128]{2,1,0:T(8,128)} %get-tuple-element.14), channel_id=1, source_target_pairs={{8,0},{16,8},{24,16},{0,24},{9,1},{17,9},{25,17},{1,25},{10,2},{18... | collective-permute-start | bytes 1769480 | tf_op jit(solution)/shard_map/ppermute | solution.py:134
  115.2 5.8 %collective-permute-start.20 = (f32[2,72,18,1]{1,0,3,2:T(2,128)}, f32[2,72,18,1]{1,0,3,2:T(2,128)}, u32[]{:S(2)}, u32[]{:S(2)}) collective-permute-start(f32[2,72,18,1]{1,0,3,2:T(2,128)} %copy.92), channel_id=1, source_target_pairs={{1,0},{2,1},{3,2},{4,3},{5,4},{6,5},{7,6},{0,7},{9,8},{10,9},{11,1... | collective-permute-start | bytes 31112 | tf_op jit(solution)/shard_map/ppermute | solution.py:27
  117.5 17.1 %collective-permute-start.21 = (f32[2,72,18,1]{1,0,3,2:T(2,128)}, f32[2,72,18,1]{1,0,3,2:T(2,128)}, u32[]{:S(2)}, u32[]{:S(2)}) collective-permute-start(f32[2,72,18,1]{1,0,3,2:T(2,128)} %copy.94), channel_id=1, source_target_pairs={{0,1},{1,2},{2,3},{3,4},{4,5},{5,6},{6,7},{7,0},{8,9},{9,10},{10,1... | collective-permute-start | bytes 31112 | tf_op jit(solution)/shard_map/ppermute | solution.py:24
  119.8 23.2 %collective-permute-start.4 = (f32[4,24,288]{2,1,0:T(8,128)}, f32[4,24,288]{2,1,0:T(8,128)}, u32[]{:S(2)}, u32[]{:S(2)}) collective-permute-start(f32[4,24,288]{2,1,0:T(8,128)} %get-tuple-element.26), channel_id=1, source_target_pairs={{0,8},{8,16},{16,24},{24,0},{1,9},{9,17},{17,25},{25,1},{2,10},{10... | collective-permute-start | bytes 331784 | tf_op jit(solution)/shard_map/ppermute | solution.py:134
  120.9 15.9 %copy-start.41 = (pred[128]{0:T(512)(128)(4,1)S(1)}, pred[128]{0:T(512)(128)(4,1)}, u32[]{:S(2)}) copy-start(pred[128]{0:T(512)(128)(4,1)} %get-tuple-element.52) | copy-start | bytes 388
  120.9 15.9 %copy-start.42 = (pred[128]{0:T(512)(128)(4,1)S(1)}, pred[128]{0:T(512)(128)(4,1)}, u32[]{:S(2)}) copy-start(pred[128]{0:T(512)(128)(4,1)} %get-tuple-element.53) | copy-start | bytes 388
  120.9 22.1 %collective-permute-start.5 = (f32[4,24,288]{2,1,0:T(8,128)}, f32[4,24,288]{2,1,0:T(8,128)}, u32[]{:S(2)}, u32[]{:S(2)}) collective-permute-start(f32[4,24,288]{2,1,0:T(8,128)} %get-tuple-element.27), channel_id=1, source_target_pairs={{8,0},{16,8},{24,16},{0,24},{9,1},{17,9},{25,17},{1,25},{10,2},{18... | collective-permute-start | bytes 331784 | tf_op jit(solution)/shard_map/ppermute | solution.py:134
  (35 other events, 75.9 us)
where the time goes:
time: 172 us; the launch traced here: 170 us
  local copies, waits for them, and re-layouts  77.6 us (45%)
  starting transfers between devices  35.5 us (21%)
  other arithmetic  25.3 us (15%)
  Pallas kernels  17.8 us (10%)
  waiting for transfers between devices  7.07 us (4%)
  matrix products  5.73 us (3%)
    pallas_call x1, Pallas kernels, transport(): pl.pallas_call(functools.partial(transport_kernel, elem_rows, levels), ou...  17.8 us
    ppermute x3, starting transfers between devices, shift_both(): lax.ppermute(backward_piece, axis, backward)  15 us
    slice x8, local copies, waits for them, and re-layouts, padded_2(): lax.slice_in_dim(block, 0, width, axis=dim)  15 us
    select_n x4, other arithmetic, edge_average(): jnp.where(column_mod == 3, 0.5 * (middle + padded[..., 2:]), jnp.where(co...  12.4 us
    ppermute x8, starting transfers between devices, padded_2(): lax.ppermute(lax.slice_in_dim(block, 0, width, axis=dim), axis, backward)  12.2 us
    slice x6, local copies, waits for them, and re-layouts, padded_2(): lax.slice_in_dim(block, block.shape[dim] - width, None, axis=dim)  9.24 us
    ppermute x4, local copies, waits for them, and re-layouts, padded_2(): lax.ppermute(lax.slice_in_dim(block, 0, width, axis=dim), axis, backward)  8.19 us
    ppermute x4, local copies, waits for them, and re-layouts, padded_2(): lax.ppermute(lax.slice_in_dim(block, block.shape[dim] - width, None, axis...  8.15 us
  transfers between devices with their start and end apart: 22, of which 4 were waited for; matrix products, arithmetic and copies ran while one was open for 58% of the time, Pallas kernels for 0%

commit v1 on v0

--- a/solution.py
+++ b/solution.py
@@ -13,20 +13,6 @@
 RX = 3
 RY = 1
 OFFS = 64
-
-
-def padded_2(block, sides, width):
-    for axis, dim in sides:
-        count = lax.axis_size(axis)
-        forward = [(i, i + 1) for i in range(count - 1)]
-        forward.append((count - 1, 0))
-        backward = [(target, source) for source, target in forward]
-        low = lax.ppermute(
-            lax.slice_in_dim(block, block.shape[dim] - width, None, axis=dim), axis, forward
-        )
-        high = lax.ppermute(lax.slice_in_dim(block, 0, width, axis=dim), axis, backward)
-        block = jnp.concatenate([low, block, high], axis=dim)
-    return block
 
 
 def gll_points():
@@ -67,56 +53,195 @@
     return jnp.stack(values_list, axis=-1)
 
 
-def along_columns(field):
-    count = field.shape[-1] // 4
-    matrix = jnp.asarray(np.kron(np.eye(count), derivative().T), jnp.float32)
-    return jnp.matmul(field, matrix, precision=lax.Precision.HIGHEST)
-
-
-def along_rows(field):
-    count = field.shape[-2] // 4
-    matrix = jnp.asarray(np.kron(np.eye(count), derivative()), jnp.float32)
-    return jnp.einsum("ij,...jq->...iq", matrix, field, precision=lax.Precision.HIGHEST)
-
-
-def edge_average(padded):
-    inner_cols = padded.shape[-1] - 2
-    column_mod = lax.broadcasted_iota(jnp.int32, (inner_cols,), 0) % 4
-    middle = padded[..., 1:-1]
-    across = jnp.where(
-        column_mod == 3,
-        0.5 * (middle + padded[..., 2:]),
-        jnp.where(column_mod == 0, 0.5 * (middle + padded[..., :-2]), middle),
+def roll_table():
+    table = derivative()
+    shifts = np.zeros((7, 4))
+    for target in range(4):
+        for source in range(4):
+            shifts[source - target + 3, target] = table[target, source]
+    return shifts
+
+
+def apply_shifts(field, table, axis):
+    size = field.shape[axis]
+    total = field * table[3][None]
+    for k in (-3, -2, -1, 1, 2, 3):
+        total = total + pltpu.roll(field, (-k) % size, axis) * table[k + 3][None]
+    return total
+
+
+def wave_kernel(
+    thickness, winds, rate, by_col, by_row, take, put, height, winds_out,
+    fresh, across, side, col_send, col_recv, row_send, row_recv, send_sem, recv_sem,
+):
+    levels, rows, cols = thickness.shape
+    chunk = 8
+    neighbours = []
+    for axis in ("elem", "face"):
+        count = lax.axis_size(axis)
+        here = lax.axis_index(axis)
+        neighbours.append((axis, lax.rem(here + 1, count), lax.rem(here + count - 1, count)))
+    barrier = pltpu.get_barrier_semaphore()
+    for axis, up, down in neighbours:
+        for place in (up, down):
+            pl.semaphore_signal(
+                barrier, inc=1, device_id={axis: place}, device_id_type=pl.DeviceIdType.MESH
+            )
+    pl.semaphore_wait(barrier, 4)
+
+    lane = lax.broadcasted_iota(jnp.int32, (rows, cols), 1)
+    line = lax.broadcasted_iota(jnp.int32, (rows, cols), 0)
+
+    def masks(position, size):
+        later = jnp.where((position % 4 == 3) & (position != size - 1), 0.5, 0.0)
+        earlier = jnp.where((position % 4 == 0) & (position != 0), 0.5, 0.0)
+        own = jnp.where((position % 4 == 0) | (position % 4 == 3), 0.5, 1.0)
+        return own[None], later[None], earlier[None]
+
+    def exchange(number, which, sources, targets):
+        axis, up, down = neighbours[which]
+        copies = []
+        for way, place in ((0, up), (1, down)):
+            copies.append(
+                pltpu.make_async_remote_copy(
+                    src_ref=sources[way],
+                    dst_ref=targets[way],
+                    send_sem=send_sem.at[number, which, way],
+                    recv_sem=recv_sem.at[number, which, way],
+                    device_id={axis: place},
+                    device_id_type=pl.DeviceIdType.MESH,
+                )
+            )
+        for copy in copies:
+            copy.start()
+        for copy in copies:
+            copy.wait()
+
+    def average(number, count, store):
+        edges = None
+        for f in range(count):
+            flat = fresh[f].reshape(levels * rows, cols)
+            term = lax.dot_general(
+                take[f], flat, (((1,), (1,)), ((), ())),
+                precision=lax.Precision.HIGHEST, preferred_element_type=jnp.float32,
+            )
+            edges = term if edges is None else edges + term
+        col_send[number] = edges
+        exchange(
+            number, 0,
+            (col_send.at[number], col_send.at[number]),
+            (col_recv.at[number, 0], col_recv.at[number, 1]),
+        )
+        both = jnp.concatenate([col_recv[number, 0], col_recv[number, 1]], axis=0)
+        own, later, earlier = masks(lane, cols)
+        for f in range(count):
+            spread = lax.dot_general(
+                both, put[f], (((0,), (0,)), ((), ())),
+                precision=lax.Precision.HIGHEST, preferred_element_type=jnp.float32,
+            )
+            side[f] = spread.reshape(levels, rows, cols)
+
+            @pl.loop(0, levels // chunk)
+            def _(step, f=f):
+                at = pl.ds(pl.multiple_of(step * chunk, chunk), chunk)
+                field = fresh[f, at]
+                mixed = field * own + pltpu.roll(field, cols - 1, 2) * later
+                mixed = mixed + pltpu.roll(field, 1, 2) * earlier + side[f, at]
+                across[f, at] = mixed
+                row_send[number, 0, f, at, :] = mixed[:, rows - 1, :]
+                row_send[number, 1, f, at, :] = mixed[:, 0, :]
+
+        exchange(
+            number, 1,
+            (row_send.at[number, 0, pl.ds(0, count)], row_send.at[number, 1, pl.ds(0, count)]),
+            (row_recv.at[number, 0, pl.ds(0, count)], row_recv.at[number, 1, pl.ds(0, count)]),
+        )
+        own_row, later_row, earlier_row = masks(line, rows)
+        first = jnp.where(line == 0, 0.5, 0.0)[None]
+        last = jnp.where(line == rows - 1, 0.5, 0.0)[None]
+        for f in range(count):
+
+            @pl.loop(0, levels // chunk)
+            def _(step, f=f):
+                at = pl.ds(pl.multiple_of(step * chunk, chunk), chunk)
+                field = across[f, at]
+                mixed = field * own_row + pltpu.roll(field, rows - 1, 1) * later_row
+                mixed = mixed + pltpu.roll(field, 1, 1) * earlier_row
+                mixed = mixed + first * row_recv[number, 0, f, at, :][:, None, :]
+                mixed = mixed + last * row_recv[number, 1, f, at, :][:, None, :]
+                store(f, at, mixed)
+
+    def store_height(f, at, value):
+        height[at] = value
+
+    def store_winds(f, at, value):
+        winds_out[f, at] = value
+
+    for substep in range(SUBSTEPS):
+        old_height = thickness if substep == 0 else height
+        old_winds = winds if substep == 0 else winds_out
+
+        @pl.loop(0, levels // chunk)
+        def _(step):
+            at = pl.ds(pl.multiple_of(step * chunk, chunk), chunk)
+            flow = apply_shifts(old_winds[0, at], by_col, 2) + apply_shifts(old_winds[1, at], by_row, 1)
+            fresh[0, at] = old_height[at] - rate[at] * flow
+
+        average(2 * substep, 1, store_height)
+
+        @pl.loop(0, levels // chunk)
+        def _(step):
+            at = pl.ds(pl.multiple_of(step * chunk, chunk), chunk)
+            now = height[at]
+            fresh[0, at] = old_winds[0, at] - rate[at] * apply_shifts(now, by_col, 2)
+            fresh[1, at] = old_winds[1, at] - rate[at] * apply_shifts(now, by_row, 1)
+
+        average(2 * substep + 1, 2, store_winds)
+
+
+def waves(thickness, winds, wave_coef):
+    levels, rows, cols = thickness.shape
+    shifts = roll_table()
+    by_col = jnp.asarray(np.broadcast_to(np.tile(shifts, (1, cols // 4))[:, None, :], (7, rows, cols)), jnp.float32)
+    by_row = jnp.asarray(np.broadcast_to(np.tile(shifts, (1, rows // 4))[:, :, None], (7, rows, cols)), jnp.float32)
+    take = np.zeros((2, 8, cols))
+    put = np.zeros((2, 16, cols))
+    for f in range(2):
+        take[f, 2 * f, 0] = 1.0
+        take[f, 2 * f + 1, cols - 1] = 1.0
+        put[f, 2 * f + 1, 0] = 0.5
+        put[f, 8 + 2 * f, cols - 1] = 0.5
+    rate = jnp.broadcast_to(wave_coef[:, None, None], (levels, 1, cols))
+    rounds = 2 * SUBSTEPS
+    wide = levels * rows
+    return pl.pallas_call(
+        wave_kernel,
+        out_shape=(
+            jax.ShapeDtypeStruct(thickness.shape, jnp.float32),
+            jax.ShapeDtypeStruct(winds.shape, jnp.float32),
+        ),
+        in_specs=[pl.BlockSpec(memory_space=pltpu.VMEM)] * 7,
+        out_specs=(pl.BlockSpec(memory_space=pltpu.VMEM), pl.BlockSpec(memory_space=pltpu.VMEM)),
+        scratch_shapes=[
+            pltpu.VMEM(winds.shape, jnp.float32),
+            pltpu.VMEM(winds.shape, jnp.float32),
+            pltpu.VMEM(winds.shape, jnp.float32),
+            pltpu.VMEM((rounds, 8, wide), jnp.float32),
+            pltpu.VMEM((rounds, 2, 8, wide), jnp.float32),
+            pltpu.VMEM((rounds, 2, 2, levels, cols), jnp.float32),
+            pltpu.VMEM((rounds, 2, 2, levels, cols), jnp.float32),
+            pltpu.SemaphoreType.DMA((rounds, 2, 2)),
+            pltpu.SemaphoreType.DMA((rounds, 2, 2)),
+        ],
+        compiler_params=pltpu.CompilerParams(
+            collective_id=0, has_side_effects=True, vmem_limit_bytes=40 * 1024 * 1024
+        ),
+        cost_estimate=pl.CostEstimate(flops=300000000, bytes_accessed=60000000, transcendentals=0),
+        name="waves",
+    )(
+        thickness, winds, rate, by_col, by_row,
+        jnp.asarray(take, jnp.float32), jnp.asarray(put, jnp.float32),
     )
-    inner_rows = across.shape[-2] - 2
-    row_mod = lax.broadcasted_iota(jnp.int32, (inner_rows, 1), 0) % 4
-    centre = across[..., 1:-1, :]
-    return jnp.where(
-        row_mod == 3,
-        0.5 * (centre + across[..., 2:, :]),
-        jnp.where(row_mod == 0, 0.5 * (centre + across[..., :-2, :]), centre),
-    )
-
-
-def height_rim(field):
-    return padded_2(field, (("face", 1), ("elem", 2)), 1)
-
-
-def wind_rim(field):
-    return padded_2(field, (("face", 2), ("elem", 3)), 1)
-
-
-def wave_substep(height, winds_now, wave_rate, height_pad, wind_pad):
-    height = edge_average(
-        height_pad(height - wave_rate * (along_columns(winds_now[0]) + along_rows(winds_now[1])))
-    )
-    pushed = jnp.stack(
-        [
-            winds_now[0] - wave_rate * along_columns(height),
-            winds_now[1] - wave_rate * along_rows(height),
-        ]
-    )
-    return (height, edge_average(wind_pad(pushed)))
 
 
 def node_weights(offsets):
@@ -239,11 +364,7 @@
 
 
 def body(tracers, thickness, winds, wave_coef, depart, offsets):
-    wave_rate = wave_coef[:, None, None]
-    height = thickness
-    winds_now = winds
-    for substep in range(SUBSTEPS):
-        height, winds_now = wave_substep(height, winds_now, wave_rate, height_rim, wind_rim)
+    height, winds_now = waves(thickness, winds, wave_coef)
     return (transport(tracers, height, depart, offsets), height, winds_now)
 
 

time: 172 us -> 134 us (0.78)
  Pallas kernels: 17.8 us -> 84 us
  local copies, waits for them, and re-layouts: 77.6 us -> 30 us
  starting transfers between devices: 35.5 us -> 11.7 us
  other arithmetic: 25.3 us -> 1.83 us
  matrix products: 5.73 us -> 0 us
  waiting for transfers between devices: 7.07 us -> 4.85 us
    pallas_call x0 -> x1, Pallas kernels: none -> 66 us  [waves(): pl.pallas_call(wave_kernel, out_shape=(jax.ShapeDtypeStruct(thickness.sha...]
    slice x15 -> x0, local copies, waits for them, and re-layouts: 26.5 us -> none  [the longest x8 15 us: padded_2(): lax.slice_in_dim(block, 0, width, axis=dim)]
    ppermute x16 -> x0, starting transfers between devices: 19.4 us -> none  [the longest x8 12.2 us: padded_2(): lax.ppermute(lax.slice_in_dim(block, 0, width, axis=dim), axis, backward)]
    ppermute x8 -> x0, local copies, waits for them, and re-layouts: 16.3 us -> none  [the longest x4 8.19 us: padded_2(): lax.ppermute(lax.slice_in_dim(block, 0, width, axis=dim), axis, backward)]
    select_n x8 -> x0, other arithmetic: 14.2 us -> none  [the longest x4 12.4 us: edge_average(): jnp.where(column_mod == 3, 0.5 * (middle + padded[..., 2:]), jnp.where(co...]
    ppermute x16 -> x0, waiting for transfers between devices: 7.06 us -> none  [the longest x8 7.03 us: padded_2(): lax.ppermute(lax.slice_in_dim(block, block.shape[dim] - width, None, axis...]
    ppermute x3, starting transfers between devices: 15 us -> 8.73 us  [shift_both(): lax.ppermute(backward_piece, axis, backward)]
    dot_general x8 -> x0, matrix products: 5.73 us -> none  [the longest x4 3.16 us: along_columns(): return jnp.matmul(field, matrix, precision=lax.Precision.HIGHEST)]
  transfers between devices with their start and end apart: 22 -> 6, of which waited for: 4 -> 2; matrix products, arithmetic and copies ran while one was open for 58% -> 12% of each run, Pallas kernels for 0% -> 50%
where the time goes in v1:
time: 134 us; the launch traced here: 133 us
  Pallas kernels  84 us (63%)
  local copies, waits for them, and re-layouts  30 us (22%)
  starting transfers between devices  11.7 us (9%)
  waiting for transfers between devices  4.85 us (4%)
  other arithmetic  1.83 us (1%)
    pallas_call x1, Pallas kernels, waves(): pl.pallas_call(wave_kernel, out_shape=(jax.ShapeDtypeStruct(thickness.sha...  66 us
    pallas_call x1, Pallas kernels, transport(): pl.pallas_call(functools.partial(transport_kernel, elem_rows, levels), ou...  18 us
    unnamed x27, local copies, waits for them, and re-layouts  8.89 us
    ppermute x3, starting transfers between devices, shift_both(): lax.ppermute(backward_piece, axis, backward)  8.73 us
    transpose x2, local copies, waits for them, and re-layouts, transport(): rows_first[:, :, -edge:].transpose(0, 2, 1)  6.32 us
    ppermute x3, waiting for transfers between devices, shift_both(): lax.ppermute(forward_piece, axis, forward)  4.45 us
    transpose x1, local copies, waits for them, and re-layouts, transport(): jnp.pad(sides, ((0, 0), (0, node_cols - 2 * edge), (0, 0)))  4.06 us
    transpose x1, local copies, waits for them, and re-layouts, transport(): rows_first[:, :, :edge].transpose(0, 2, 1)  3.37 us
  transfers between devices with their start and end apart: 6, of which 2 were waited for; matrix products, arithmetic and copies ran while one was open for 12% of the time, Pallas kernels for 50%

profile of v1, /device:TPU:0, one launch (start us, length us, event | category | flops | bytes accessed | tf_op | source)
XLA Modules:
  0.0 133.2 jit_solution(13318375951079238764)
XLA Ops:
  0.6 2.4 %copy.17 = f32[4,72,16,128]{3,1,0,2:T(8,128)S(1)} copy(f32[4,72,16,128]{3,2,1,0:T(8,128)} %param.10) | data formatting | bytes 4718592 | tf_op args[0]
  3.1 3.0 %slice_bitcast_fusion.1 = (f32[16,12,288]{1,2,0:T(8,128)}, f32[16,12,288]{1,2,0:T(8,128)}) fusion(f32[16,288,128]{2,1,0:T(8,128)S(1)} %bitcast.32), kind=kLoop, calls=%fused_computation.2 | loop fusion | bytes 884736 | tf_op jit(solution)/shard_map/transpose | solution.py:328
  6.1 3.3 %copy.18 = f32[16,12,288]{2,0,1:T(8,128)} copy(f32[16,12,288]{1,2,0:T(8,128)} %get-tuple-element.7) | data formatting | bytes 442368 | tf_op jit(solution)/shard_map/transpose | solution.py:328
  9.4 0.5 collective-permute-start.2
  9.9 3.4 %copy.19 = f32[16,12,288]{2,0,1:T(8,128)} copy(f32[16,12,288]{1,2,0:T(8,128)} %get-tuple-element.8) | data formatting | bytes 442368 | tf_op jit(solution)/shard_map/transpose | solution.py:328
  13.2 2.9 %collective-permute-start.3 = (f32[16,12,288]{2,0,1:T(8,128)}, f32[16,12,288]{2,0,1:T(8,128)}, u32[]{:S(2)}, u32[]{:S(2)}) collective-permute-start(f32[16,12,288]{2,0,1:T(8,128)} %copy.19), channel_id=1, source_target_pairs={{1,0},{2,1},{3,2},{4,3},{5,4},{6,5},{7,6},{0,7},{9,8},{10,9},{11,1... | collective-permute-start | bytes 663560 | tf_op jit(solution)/shard_map/ppermute | solution.py:259
  16.1 1.1 fusion.19
  17.3 2.3 %collective-permute-start = (f32[4,288,128]{2,1,0:T(8,128)}, f32[4,288,128]{2,1,0:T(8,128)}, u32[]{:S(2)}, u32[]{:S(2)}) collective-permute-start(f32[4,288,128]{2,1,0:T(8,128)} %get-tuple-element.10), channel_id=1, source_target_pairs={{0,8},{8,16},{16,24},{24,0},{1,9},{9,17},{17,25},{25,1},{2,10},{10... | collective-permute-start | bytes 1769480 | tf_op jit(solution)/shard_map/ppermute | solution.py:259
  19.6 2.0 %collective-permute-start.1 = (f32[4,288,128]{2,1,0:T(8,128)}, f32[4,288,128]{2,1,0:T(8,128)}, u32[]{:S(2)}, u32[]{:S(2)}) collective-permute-start(f32[4,288,128]{2,1,0:T(8,128)} %get-tuple-element.9), channel_id=1, source_target_pairs={{8,0},{16,8},{24,16},{0,24},{9,1},{17,9},{25,17},{1,25},{10,2},{18... | collective-permute-start | bytes 1769480 | tf_op jit(solution)/shard_map/ppermute | solution.py:259
  21.9 0.1 mul.239
  22.1 0.1 reshape.356
  22.2 0.7 broadcast_multiply_fusion
  22.9 0.1 broadcast_in_dim.16.rate
  23.0 1.3 copy-done.2
  24.3 0.8 copy-done.5
  25.1 0.8 copy-done.6
  26.0 0.7 copy-done.8
  26.6 66.0 %waves.1 = (f32[72,16,128]{2,1,0:T(8,128)S(1)}, f32[2,72,16,128]{3,2,1,0:T(8,128)S(1)}) custom-call(f32[72,16,128]{2,1,0:T(8,128)S(1)} %copy-done.3, f32[2,72,16,128]{3,2,1,0:T(8,128)S(1)} %copy-done.2, f32[72,1,128]{2,1,0:T(1,128)S(1)} %broadcast_in_dim.16.rate, f32[7,16,128]{2,1,0:T(8,128)S(1)} %copy-done.5, f32[7,16,128]{2,1,0:T(8,128)S(1)} %copy-done.6, ...), custom_call_target="tpu_custom_call" | custom-call | flops 300000000 | bytes 60000000 | tf_op jit(solution)/shard_map/waves/pallas_call | solution.py:217
  92.7 1.0 copy-done
  93.7 0.2 copy.25
  93.9 1.1 copy.20
  94.9 1.1 copy.21
  96.0 0.2 collective-permute-start.4
  96.3 3.8 %collective-permute-start.5 = (f32[4,24,288]{2,1,0:T(8,128)S(1)}, f32[4,24,288]{2,1,0:T(8,128)S(1)}, u32[]{:S(2)}, u32[]{:S(2)}) collective-permute-start(f32[4,24,288]{2,1,0:T(8,128)S(1)} %get-tuple-element.12), channel_id=1, source_target_pairs={{8,0},{16,8},{24,16},{0,24},{9,1},{17,9},{25,17},{1,25},{10,2},{18... | collective-permute-start | bytes 331784 | tf_op jit(solution)/shard_map/ppermute | solution.py:259
  100.1 4.4 %collective-permute-done.4 = f32[4,24,288]{2,1,0:T(8,128)S(1)} collective-permute-done((f32[4,24,288]{2,1,0:T(8,128)S(1)}, f32[4,24,288]{2,1,0:T(8,128)S(1)}, u32[]{:S(2)}, u32[]{:S(2)}) %collective-permute-start.4) | collective-permute-done | bytes 110624 | tf_op jit(solution)/shard_map/ppermute | solution.py:259
  104.6 0.4 collective-permute-done.5
  105.0 1.0 pad_maximum_fusion
  105.9 3.3 %copy.22 = f32[24,24,288]{1,2,0:T(8,128)} copy(f32[24,24,288]{2,1,0:T(8,128)} %pad_maximum_fusion) | data formatting | bytes 1327104 | tf_op jit(solution)/shard_map/concatenate | solution.py:332
  109.3 4.1 %pad_bitcast_fusion.halo = f32[24,288,128]{2,1,0:T(8,128)} fusion(f32[24,24,288]{1,2,0:T(8,128)} %copy.22), kind=kLoop, calls=%fused_computation | loop fusion | bytes 4202496 | tf_op jit(solution)/shard_map/transpose | solution.py:333
  113.4 18.0 %transport.1 = f32[288,16,128]{2,1,0:T(8,128)} custom-call(f32[4,288,128]{2,1,0:T(8,128)} %collective-permute-done.low, f32[16,288,128]{2,1,0:T(8,128)S(1)} %bitcast.34, f32[4,288,128]{2,1,0:T(8,128)} %collective-permute-done.1.high, f32[24,288,128]{2,1,0:T(8,128)} %pad_bitcast_fusion.halo, s32[4,512]{1,0:T(4,128)S(1)} %pad_add_fusion.target, ...), custom_call_target="tpu_custom_call" | custom-call | tf_op jit(solution)/shard_map/transport/pallas_call | solution.py:351
  131.4 0.8 copy.28
  132.2 1.0 copy.29
  (34 shorter events, 0.4 us)
Async XLA Ops:
  9.4 84.5 %collective-permute-start.2 = (f32[16,12,288]{2,0,1:T(8,128)}, f32[16,12,288]{2,0,1:T(8,128)}, u32[]{:S(2)}, u32[]{:S(2)}) collective-permute-start(f32[16,12,288]{2,0,1:T(8,128)} %copy.18), channel_id=1, source_target_pairs={{0,1},{1,2},{2,3},{3,4},{4,5},{5,6},{6,7},{7,0},{8,9},{9,10},{10,1... | collective-permute-start | bytes 663560 | tf_op jit(solution)/shard_map/ppermute | solution.py:259
  9.8 11.8 %copy-start.9 = (s32[2,16,128]{2,1,0:T(8,128)S(1)}, s32[2,16,128]{2,1,0:T(8,128)}, u32[]{:S(2)}) copy-start(s32[2,16,128]{2,1,0:T(8,128)} %param.15) | copy-start | bytes 49156
  9.8 11.9 %copy-start.10 = (s32[4,32]{1,0:T(4,128)S(1)}, s32[4,32]{1,0:T(4,128)}, u32[]{:S(2)}) copy-start(s32[4,32]{1,0:T(4,128)} %param.14) | copy-start | bytes 1540
  9.8 13.0 %copy-start.11 = (f32[72]{0:T(128)S(1)}, f32[72]{0:T(128)}, u32[]{:S(2)}) copy-start(f32[72]{0:T(128)} %param.13) | copy-start | bytes 868
  9.8 13.2 %copy-start.3 = (f32[72,16,128]{2,1,0:T(8,128)S(1)}, f32[72,16,128]{2,1,0:T(8,128)}, u32[]{:S(2)}) copy-start(f32[72,16,128]{2,1,0:T(8,128)} %thickness.1) | copy-start | bytes 1769476
  9.8 13.2 %copy-start.7 = (f32[2,16,128]{2,1,0:T(8,128)S(1)}, f32[2,16,128]{2,1,0:T(8,128)}, u32[]{:S(2)}) copy-start(f32[2,16,128]{2,1,0:T(8,128)} %constant.162.clone.put) | copy-start | bytes 49156
  13.2 81.7 %collective-permute-start.3 = (f32[16,12,288]{2,0,1:T(8,128)}, f32[16,12,288]{2,0,1:T(8,128)}, u32[]{:S(2)}, u32[]{:S(2)}) collective-permute-start(f32[16,12,288]{2,0,1:T(8,128)} %copy.19), channel_id=1, source_target_pairs={{1,0},{2,1},{3,2},{4,3},{5,4},{6,5},{7,6},{0,7},{9,8},{10,9},{11,1... | collective-permute-start | bytes 663560 | tf_op jit(solution)/shard_map/ppermute | solution.py:259
  17.3 96.1 %collective-permute-start = (f32[4,288,128]{2,1,0:T(8,128)}, f32[4,288,128]{2,1,0:T(8,128)}, u32[]{:S(2)}, u32[]{:S(2)}) collective-permute-start(f32[4,288,128]{2,1,0:T(8,128)} %get-tuple-element.10), channel_id=1, source_target_pairs={{0,8},{8,16},{16,24},{24,0},{1,9},{9,17},{17,25},{25,1},{2,10},{10... | collective-permute-start | bytes 1769480 | tf_op jit(solution)/shard_map/ppermute | solution.py:259
  19.6 93.7 %collective-permute-start.1 = (f32[4,288,128]{2,1,0:T(8,128)}, f32[4,288,128]{2,1,0:T(8,128)}, u32[]{:S(2)}, u32[]{:S(2)}) collective-permute-start(f32[4,288,128]{2,1,0:T(8,128)} %get-tuple-element.9), channel_id=1, source_target_pairs={{8,0},{16,8},{24,16},{0,24},{9,1},{17,9},{25,17},{1,25},{10,2},{18... | collective-permute-start | bytes 1769480 | tf_op jit(solution)/shard_map/ppermute | solution.py:259
  23.0 1.3 copy-start.2
  24.3 0.8 copy-start.5
  25.1 0.8 copy-start.6
  25.9 0.7 copy-start.8
  92.6 1.0 copy-start
  96.0 8.5 %collective-permute-start.4 = (f32[4,24,288]{2,1,0:T(8,128)S(1)}, f32[4,24,288]{2,1,0:T(8,128)S(1)}, u32[]{:S(2)}, u32[]{:S(2)}) collective-permute-start(f32[4,24,288]{2,1,0:T(8,128)S(1)} %get-tuple-element.11), channel_id=1, source_target_pairs={{0,8},{8,16},{16,24},{24,0},{1,9},{9,17},{17,25},{25,1},{2,10},{10... | collective-permute-start | bytes 331784 | tf_op jit(solution)/shard_map/ppermute | solution.py:259
  96.3 8.7 %collective-permute-start.5 = (f32[4,24,288]{2,1,0:T(8,128)S(1)}, f32[4,24,288]{2,1,0:T(8,128)S(1)}, u32[]{:S(2)}, u32[]{:S(2)}) collective-permute-start(f32[4,24,288]{2,1,0:T(8,128)S(1)} %get-tuple-element.12), channel_id=1, source_target_pairs={{8,0},{16,8},{24,16},{0,24},{9,1},{17,9},{25,17},{1,25},{10,2},{18... | collective-permute-start | bytes 331784 | tf_op jit(solution)/shard_map/ppermute | solution.py:259
  109.3 4.1 %copy-start.4 = (f32[16,128,4,4]{1,0,3,2:T(8,128)S(1)}, f32[16,128,4,4]{1,0,3,2:T(8,128)}, u32[]{:S(2)}) copy-start(f32[16,128,4,4]{1,0,3,2:T(8,128)} %broadcast_multiply_fusion) | copy-start | bytes 393220
  113.3 18.8 %copy-start.1 = (f32[2,72,16,128]{3,2,1,0:T(8,128)S(1)}, f32[2,72,16,128]{3,2,1,0:T(8,128)}, u32[]{:S(2)}) copy-start(f32[2,72,16,128]{3,2,1,0:T(8,128)} %copy-done) | copy-start | bytes 3538948

commit v2 on v1

--- a/solution.py
+++ b/solution.py
@@ -70,6 +70,21 @@
     return total
 
 
+def selected(table, values, dim, values_first):
+    table = table.astype(jnp.bfloat16)
+    total = None
+    rest = values
+    for _ in range(3):
+        piece = rest.astype(jnp.bfloat16)
+        rest = rest - piece.astype(jnp.float32)
+        pair = (piece, table) if values_first else (table, piece)
+        term = lax.dot_general(
+            *pair, (((dim,), (dim,)), ((), ())), preferred_element_type=jnp.float32
+        )
+        total = term if total is None else total + term
+    return total
+
+
 def wave_kernel(
     thickness, winds, rate, by_col, by_row, take, put, height, winds_out,
     fresh, across, side, col_send, col_recv, row_send, row_recv, send_sem, recv_sem,
@@ -121,10 +136,7 @@
         edges = None
         for f in range(count):
             flat = fresh[f].reshape(levels * rows, cols)
-            term = lax.dot_general(
-                take[f], flat, (((1,), (1,)), ((), ())),
-                precision=lax.Precision.HIGHEST, preferred_element_type=jnp.float32,
-            )
+            term = selected(take[f], flat, 1, False)
             edges = term if edges is None else edges + term
         col_send[number] = edges
         exchange(
@@ -135,10 +147,7 @@
         both = jnp.concatenate([col_recv[number, 0], col_recv[number, 1]], axis=0)
         own, later, earlier = masks(lane, cols)
         for f in range(count):
-            spread = lax.dot_general(
-                both, put[f], (((0,), (0,)), ((), ())),
-                precision=lax.Precision.HIGHEST, preferred_element_type=jnp.float32,
-            )
+            spread = selected(put[f], both, 0, True)
             side[f] = spread.reshape(levels, rows, cols)
 
             @pl.loop(0, levels // chunk)
@@ -312,7 +321,7 @@
                 out[pl.ds(start, chunk), row, :] = value * height[row, pl.ds(level, chunk), :]
 
 
-def transport(tracers, height, depart, offsets):
+def step(tracers, thickness, winds, wave_coef, depart, offsets):
     count, levels, node_rows, node_cols = tracers.shape
     elem_rows = node_rows // 4
     elem_cols = node_cols // 4
@@ -322,7 +331,6 @@
     grid_rows = elem_rows * lax.axis_size("face")
     grid_cols = elem_cols * lax.axis_size("elem")
     rows_first = tracers.reshape(channels, node_rows, node_cols).transpose(1, 0, 2)
-    low, high = shift_both(rows_first[-4:], rows_first[:4], "face")
     edge = 4 * RX
     left, right = shift_both(
         rows_first[:, :, -edge:].transpose(0, 2, 1), rows_first[:, :, :edge].transpose(0, 2, 1), "elem"
@@ -331,6 +339,9 @@
     under, above = shift_both(sides[-4:], sides[:4], "face")
     sides = jnp.concatenate([under, sides, above], axis=0)
     halo = jnp.pad(sides, ((0, 0), (0, node_cols - 2 * edge), (0, 0))).transpose(0, 2, 1)
+    halo, rows_first, thickness, winds = lax.optimization_barrier((halo, rows_first, thickness, winds))
+    low, high = shift_both(rows_first[-4:], rows_first[:4], "face")
+    height, new_winds = waves(thickness, winds, wave_coef)
 
     row_index = lax.broadcasted_iota(jnp.int32, (elem_rows, elem_cols), 0)
     col_index = lax.broadcasted_iota(jnp.int32, (elem_rows, elem_cols), 1)
@@ -360,12 +371,7 @@
         compiler_params=pltpu.CompilerParams(vmem_limit_bytes=48 * 1024 * 1024),
         name="transport",
     )(low, rows_first, high, halo, target, weights, height.transpose(1, 0, 2))
-    return out.reshape(tracers.shape)
-
-
-def body(tracers, thickness, winds, wave_coef, depart, offsets):
-    height, winds_now = waves(thickness, winds, wave_coef)
-    return (transport(tracers, height, depart, offsets), height, winds_now)
+    return (out.reshape(tracers.shape), height, new_winds)
 
 
 def solution(mesh):
@@ -382,4 +388,4 @@
         P(None, "face", "elem"),
         P(None, None, "face", "elem"),
     )
-    return jax.shard_map(body, mesh=mesh, in_specs=in_specs, out_specs=out_specs, check_vma=False)
+    return jax.shard_map(step, mesh=mesh, in_specs=in_specs, out_specs=out_specs, check_vma=False)

time: 134 us -> 132 us (0.985)
  local copies, waits for them, and re-layouts: 30 us -> 24.7 us
  Pallas kernels: 84 us -> 86.5 us
  starting transfers between devices: 11.7 us -> 9.69 us
  other arithmetic: 1.83 us -> 3.44 us
    unnamed x27 -> x17, local copies, waits for them, and re-layouts: 8.89 us -> 4.29 us
    pallas_call x1, Pallas kernels: 66 us -> 68.9 us  [waves(): pl.pallas_call(wave_kernel, out_shape=(jax.ShapeDtypeStruct(thickness.sha...]
    broadcast_in_dim x2, local copies, waits for them, and re-layouts: 0.15 us -> 2.1 us  [the longest x1 1.39 us: step(): which = jnp.repeat(row_shift, 4, axis=1)]
    transpose x4, local copies, waits for them, and re-layouts: 13.8 us -> 12.3 us  [the longest x2 5.58 us: step(): rows_first[:, :, -edge:].transpose(0, 2, 1)]
    mul x1, local copies, waits for them, and re-layouts: 0.12 us -> 1.52 us  [step(): targets.append(which * width + spot)]
    reshape x1, local copies, waits for them, and re-layouts: 0.12 us -> 1.52 us  [step(): first = jnp.repeat(4 * (col_index + col_shift), 4, axis=1)]
  transfers between devices with their start and end apart: 6 -> 6, of which waited for: 2 -> 2; matrix products, arithmetic and copies ran while one was open for 12% -> 9% of each run, Pallas kernels for 50% -> 53%
where the time goes in v2:
time: 132 us; the launch traced here: 131 us
  Pallas kernels  86.5 us (66%)
  local copies, waits for them, and re-layouts  24.7 us (19%)
  starting transfers between devices  9.69 us (7%)
  waiting for transfers between devices  6.11 us (5%)
  other arithmetic  3.44 us (3%)
    pallas_call x1, Pallas kernels, waves(): pl.pallas_call(wave_kernel, out_shape=(jax.ShapeDtypeStruct(thickness.sha...  68.9 us
    pallas_call x1, Pallas kernels, step(): pl.pallas_call(functools.partial(transport_kernel, elem_rows, levels), ou...  17.6 us
    ppermute x3, starting transfers between devices, shift_both(): lax.ppermute(backward_piece, axis, backward)  8 us
    transpose x2, local copies, waits for them, and re-layouts, step(): rows_first[:, :, -edge:].transpose(0, 2, 1)  5.58 us
    ppermute x3, waiting for transfers between devices, shift_both(): lax.ppermute(forward_piece, axis, forward)  4.72 us
    unnamed x17, local copies, waits for them, and re-layouts  4.29 us
    transpose x1, local copies, waits for them, and re-layouts, step(): jnp.pad(sides, ((0, 0), (0, node_cols - 2 * edge), (0, 0)))  4.08 us
  transfers between devices with their start and end apart: 6, of which 2 were waited for; matrix products, arithmetic and copies ran while one was open for 9% of the time, Pallas kernels for 53%

profile of v2, /device:TPU:0, one launch (start us, length us, event | category | flops | bytes accessed | tf_op | source)
XLA Modules:
  0.0 131.3 jit_solution(4119211477503223207)
XLA Ops:
  0.6 2.4 %copy.17 = f32[4,72,16,128]{3,1,0,2:T(8,128)S(1)} copy(f32[4,72,16,128]{3,2,1,0:T(8,128)} %param.10) | data formatting | bytes 4718592 | tf_op args[0]
  3.1 3.0 %slice_bitcast_fusion.1 = (f32[16,12,288]{1,2,0:T(8,128)}, f32[16,12,288]{1,2,0:T(8,128)}) fusion(f32[16,288,128]{2,1,0:T(8,128)S(1)} %bitcast.32), kind=kLoop, calls=%fused_computation.2 | loop fusion | bytes 884736 | tf_op jit(solution)/shard_map/transpose | solution.py:336
  6.1 2.6 %copy.19 = f32[16,12,288]{2,0,1:T(8,128)S(1)} copy(f32[16,12,288]{1,2,0:T(8,128)} %get-tuple-element.18) | data formatting | bytes 442368 | tf_op jit(solution)/shard_map/transpose | solution.py:336
  8.6 3.4 %collective-permute-start.1 = (f32[16,12,288]{2,0,1:T(8,128)S(1)}, f32[16,12,288]{2,0,1:T(8,128)S(1)}, u32[]{:S(2)}, u32[]{:S(2)}) collective-permute-start(f32[16,12,288]{2,0,1:T(8,128)S(1)} %copy.19), channel_id=1, source_target_pairs={{1,0},{2,1},{3,2},{4,3},{5,4},{6,5},{7,6},{0,7},{9,8},{10,9},{11,1... | collective-permute-start | bytes 663560 | tf_op jit(solution)/shard_map/ppermute | solution.py:268
  12.0 2.6 %copy.18 = f32[16,12,288]{2,0,1:T(8,128)S(1)} copy(f32[16,12,288]{1,2,0:T(8,128)} %get-tuple-element.17) | data formatting | bytes 442368 | tf_op jit(solution)/shard_map/transpose | solution.py:336
  14.6 0.1 collective-permute-start
  14.7 0.5 iota_add_fusion.1
  15.2 0.7 multiply_add_fusion
  15.9 1.3 %fusion.9 = (s32[4,32]{1,0:T(4,128)S(1)}, s32[4,32]{1,0:T(4,128)}) fusion(s32[32]{0:T(128)S(1)} %iota_add_fusion, s32[4,32]{1,0:T(4,128)} %param.14, s32[4]{0:T(128)} %iota_add_fusion.1), kind=kLoop, calls=%fused_computation.44 | loop fusion | flops 6272 | bytes 1680 | tf_op jit(solution)/shard_map/mul | solution.py:352
  17.3 0.7 broadcast_in_dim.7
  18.0 1.5 %reshape.356 = s32[4,128]{1,0:T(4,128)} reshape(s32[4,32,4]{2,1,0:T(8,128)} %broadcast_in_dim.7) | data formatting | bytes 4096 | tf_op jit(solution)/shard_map/reshape | solution.py:352
  19.5 1.4 %broadcast_in_dim.6 = s32[4,32,4]{2,1,0:T(8,128)} broadcast(s32[4,32]{1,0:T(4,128)} %get-tuple-element.34), dimensions={0,1} | broadcast | bytes 2560 | tf_op jit(solution)/shard_map/broadcast_in_dim | solution.py:353
  20.9 1.5 %mul.239 = s32[4,128]{1,0:T(4,128)} reshape(s32[4,32,4]{2,1,0:T(8,128)} %broadcast_in_dim.6) | data formatting | bytes 4096 | tf_op jit(solution)/shard_map/mul | solution.py:359
  22.4 0.7 fusion.11
  23.1 0.1 copy.21
  23.3 0.1 copy.20
  23.4 1.6 %collective-permute-start.2 = (f32[4,24,288]{2,1,0:T(8,128)S(1)}, f32[4,24,288]{2,1,0:T(8,128)S(1)}, u32[]{:S(2)}, u32[]{:S(2)}) collective-permute-start(f32[4,24,288]{2,1,0:T(8,128)S(1)} %get-tuple-element.19), channel_id=1, source_target_pairs={{0,8},{8,16},{16,24},{24,0},{1,9},{9,17},{17,25},{25,1},{2,10},{10... | collective-permute-start | bytes 331784 | tf_op jit(solution)/shard_map/ppermute | solution.py:268
  25.1 2.2 %collective-permute-start.3 = (f32[4,24,288]{2,1,0:T(8,128)S(1)}, f32[4,24,288]{2,1,0:T(8,128)S(1)}, u32[]{:S(2)}, u32[]{:S(2)}) collective-permute-start(f32[4,24,288]{2,1,0:T(8,128)S(1)} %get-tuple-element.20), channel_id=1, source_target_pairs={{8,0},{16,8},{24,16},{0,24},{9,1},{17,9},{25,17},{1,25},{10,2},{18... | collective-permute-start | bytes 331784 | tf_op jit(solution)/shard_map/ppermute | solution.py:268
  27.3 4.7 %collective-permute-done.2 = f32[4,24,288]{2,1,0:T(8,128)S(1)} collective-permute-done((f32[4,24,288]{2,1,0:T(8,128)S(1)}, f32[4,24,288]{2,1,0:T(8,128)S(1)}, u32[]{:S(2)}, u32[]{:S(2)}) %collective-permute-start.2) | collective-permute-done | bytes 110624 | tf_op jit(solution)/shard_map/ppermute | solution.py:268
  32.0 1.4 %collective-permute-done.3 = f32[4,24,288]{2,1,0:T(8,128)S(1)} collective-permute-done((f32[4,24,288]{2,1,0:T(8,128)S(1)}, f32[4,24,288]{2,1,0:T(8,128)S(1)}, u32[]{:S(2)}, u32[]{:S(2)}) %collective-permute-start.3) | collective-permute-done | bytes 110624 | tf_op jit(solution)/shard_map/ppermute | solution.py:268
  33.4 0.1 pad_maximum_fusion
  33.5 2.4 %copy.22 = f32[24,24,288]{1,2,0:T(8,128)} copy(f32[24,24,288]{2,1,0:T(8,128)S(1)} %pad_maximum_fusion) | data formatting | bytes 1327104 | tf_op jit(solution)/shard_map/concatenate | solution.py:340
  35.9 4.1 %pad_bitcast_fusion.halo = f32[24,288,128]{2,1,0:T(8,128)} fusion(f32[24,24,288]{1,2,0:T(8,128)} %copy.22), kind=kLoop, calls=%fused_computation | loop fusion | bytes 4202496 | tf_op jit(solution)/shard_map/transpose | solution.py:341
  40.0 0.0 copy-start.3
  40.0 0.1 fusion.19
  40.1 2.4 %collective-permute-start.5 = (f32[4,288,128]{2,1,0:T(8,128)S(1)}, f32[4,288,128]{2,1,0:T(8,128)S(1)}, u32[]{:S(2)}, u32[]{:S(2)}) collective-permute-start(f32[4,288,128]{2,1,0:T(8,128)S(1)} %get-tuple-element.15), channel_id=1, source_target_pairs={{8,0},{16,8},{24,16},{0,24},{9,1},{17,9},{25,17},{1,25},{10,2},{18... | collective-permute-start | bytes 1769480 | tf_op jit(solution)/shard_map/ppermute | solution.py:268
  42.5 0.1 broadcast_in_dim.16.rate
  42.7 68.9 %waves.1 = (f32[72,16,128]{2,1,0:T(8,128)S(1)}, f32[2,72,16,128]{3,2,1,0:T(8,128)S(1)}) custom-call(f32[72,16,128]{2,1,0:T(8,128)S(1)} %copy-done.1, f32[2,72,16,128]{3,2,1,0:T(8,128)S(1)} %copy-done, f32[72,1,128]{2,1,0:T(1,128)S(1)} %broadcast_in_dim.16.rate, f32[7,16,128]{2,1,0:T(8,128)S(1)} %copy-done.3, f32[7,16,128]{2,1,0:T(8,128)S(1)} %copy-done.2, ...), custom_call_target="tpu_custom_call" | custom-call | flops 300000000 | bytes 60000000 | tf_op jit(solution)/shard_map/waves/pallas_call | solution.py:226
  111.7 0.2 copy.25
  111.9 17.6 %transport.1 = f32[288,16,128]{2,1,0:T(8,128)} custom-call(f32[4,288,128]{2,1,0:T(8,128)S(1)} %collective-permute-done.4.low, f32[16,288,128]{2,1,0:T(8,128)S(1)} %bitcast.34, f32[4,288,128]{2,1,0:T(8,128)S(1)} %collective-permute-done.5.high, f32[24,288,128]{2,1,0:T(8,128)} %pad_bitcast_fusion.halo, s32[4,512]{1,0:T(4,128)S(1)} %pad_add_fusion.target, ...), custom_call_target="tpu_custom_call" | custom-call | tf_op jit(solution)/shard_map/transport/pallas_call | solution.py:362
  129.5 0.8 copy.28
  130.3 1.0 copy.29
  (24 shorter events, 0.1 us)
Async XLA Ops:
  8.6 14.5 %collective-permute-start.1 = (f32[16,12,288]{2,0,1:T(8,128)S(1)}, f32[16,12,288]{2,0,1:T(8,128)S(1)}, u32[]{:S(2)}, u32[]{:S(2)}) collective-permute-start(f32[16,12,288]{2,0,1:T(8,128)S(1)} %copy.19), channel_id=1, source_target_pairs={{1,0},{2,1},{3,2},{4,3},{5,4},{6,5},{7,6},{0,7},{9,8},{10,9},{11,1... | collective-permute-start | bytes 663560 | tf_op jit(solution)/shard_map/ppermute | solution.py:268
  14.6 8.6 %collective-permute-start = (f32[16,12,288]{2,0,1:T(8,128)S(1)}, f32[16,12,288]{2,0,1:T(8,128)S(1)}, u32[]{:S(2)}, u32[]{:S(2)}) collective-permute-start(f32[16,12,288]{2,0,1:T(8,128)S(1)} %copy.18), channel_id=1, source_target_pairs={{0,1},{1,2},{2,3},{3,4},{4,5},{5,6},{6,7},{7,0},{8,9},{9,10},{10,1... | collective-permute-start | bytes 663560 | tf_op jit(solution)/shard_map/ppermute | solution.py:268
  23.4 8.6 %collective-permute-start.2 = (f32[4,24,288]{2,1,0:T(8,128)S(1)}, f32[4,24,288]{2,1,0:T(8,128)S(1)}, u32[]{:S(2)}, u32[]{:S(2)}) collective-permute-start(f32[4,24,288]{2,1,0:T(8,128)S(1)} %get-tuple-element.19), channel_id=1, source_target_pairs={{0,8},{8,16},{16,24},{24,0},{1,9},{9,17},{17,25},{25,1},{2,10},{10... | collective-permute-start | bytes 331784 | tf_op jit(solution)/shard_map/ppermute | solution.py:268
  25.1 8.3 %collective-permute-start.3 = (f32[4,24,288]{2,1,0:T(8,128)S(1)}, f32[4,24,288]{2,1,0:T(8,128)S(1)}, u32[]{:S(2)}, u32[]{:S(2)}) collective-permute-start(f32[4,24,288]{2,1,0:T(8,128)S(1)} %get-tuple-element.20), channel_id=1, source_target_pairs={{8,0},{16,8},{24,16},{0,24},{9,1},{17,9},{25,17},{1,25},{10,2},{18... | collective-permute-start | bytes 331784 | tf_op jit(solution)/shard_map/ppermute | solution.py:268
  39.9 2.6 %copy-start.6 = (f32[72]{0:T(128)S(1)}, f32[72]{0:T(128)}, u32[]{:S(2)}) copy-start(f32[72]{0:T(128)} %param.13) | copy-start | bytes 868
  39.9 2.7 %copy-start = (f32[2,72,16,128]{3,2,1,0:T(8,128)S(1)}, f32[2,72,16,128]{3,2,1,0:T(8,128)}, u32[]{:S(2)}) copy-start(f32[2,72,16,128]{3,2,1,0:T(8,128)} %winds) | copy-start | bytes 3538948
  39.9 2.7 %copy-start.1 = (f32[72,16,128]{2,1,0:T(8,128)S(1)}, f32[72,16,128]{2,1,0:T(8,128)}, u32[]{:S(2)}) copy-start(f32[72,16,128]{2,1,0:T(8,128)} %thickness) | copy-start | bytes 1769476
  39.9 2.7 %copy-start.2 = (f32[7,16,128]{2,1,0:T(8,128)S(1)}, f32[7,16,128]{2,1,0:T(8,128)}, u32[]{:S(2)}) copy-start(f32[7,16,128]{2,1,0:T(8,128)} %constant.160.clone.by_row) | copy-start | bytes 172036
  40.0 2.7 %copy-start.3 = (f32[7,16,128]{2,1,0:T(8,128)S(1)}, f32[7,16,128]{2,1,0:T(8,128)}, u32[]{:S(2)}) copy-start(f32[7,16,128]{2,1,0:T(8,128)} %constant.159.clone.by_col) | copy-start | bytes 172036
  40.0 2.7 %copy-start.4 = (f32[2,16,128]{2,1,0:T(8,128)S(1)}, f32[2,16,128]{2,1,0:T(8,128)}, u32[]{:S(2)}) copy-start(f32[2,16,128]{2,1,0:T(8,128)} %constant.162.clone.put) | copy-start | bytes 49156
  40.0 2.7 %copy-start.5 = (f32[2,8,128]{2,1,0:T(8,128)S(1)}, f32[2,8,128]{2,1,0:T(8,128)}, u32[]{:S(2)}) copy-start(f32[2,8,128]{2,1,0:T(8,128)} %constant.161.clone.take) | copy-start | bytes 24580
  40.1 71.8 %collective-permute-start.5 = (f32[4,288,128]{2,1,0:T(8,128)S(1)}, f32[4,288,128]{2,1,0:T(8,128)S(1)}, u32[]{:S(2)}, u32[]{:S(2)}) collective-permute-start(f32[4,288,128]{2,1,0:T(8,128)S(1)} %get-tuple-element.15), channel_id=1, source_target_pairs={{8,0},{16,8},{24,16},{0,24},{9,1},{17,9},{25,17},{1,25},{10,2},{18... | collective-permute-start | bytes 1769480 | tf_op jit(solution)/shard_map/ppermute | solution.py:268
  42.4 69.4 %collective-permute-start.4 = (f32[4,288,128]{2,1,0:T(8,128)S(1)}, f32[4,288,128]{2,1,0:T(8,128)S(1)}, u32[]{:S(2)}, u32[]{:S(2)}) collective-permute-start(f32[4,288,128]{2,1,0:T(8,128)S(1)} %get-tuple-element.16), channel_id=1, source_target_pairs={{0,8},{8,16},{16,24},{24,0},{1,9},{9,17},{17,25},{25,1},{2,10},{10... | collective-permute-start | bytes 1769480 | tf_op jit(solution)/shard_map/ppermute | solution.py:268

commit v3 on v2

--- a/solution.py
+++ b/solution.py
@@ -63,11 +63,15 @@
 
 
 def apply_shifts(field, table, axis):
+    shape = field.shape
+    if axis == 1:
+        field = field.reshape(-1, 8, shape[2])
+        table = table[:, :8]
     size = field.shape[axis]
     total = field * table[3][None]
     for k in (-3, -2, -1, 1, 2, 3):
         total = total + pltpu.roll(field, (-k) % size, axis) * table[k + 3][None]
-    return total
+    return total.reshape(shape)
 
 
 def selected(table, values, dim, values_first):

time: 132 us -> 132 us (level)
  no operation moved by 1% of the time
where the time goes in v3:
time: 132 us; the launch traced here: 131 us
  Pallas kernels  86.5 us (66%)
  local copies, waits for them, and re-layouts  24.7 us (19%)
  starting transfers between devices  9.69 us (7%)
  waiting for transfers between devices  6.11 us (5%)
  other arithmetic  3.44 us (3%)
    pallas_call x1, Pallas kernels, waves(): pl.pallas_call(wave_kernel, out_shape=(jax.ShapeDtypeStruct(thickness.sha...  68.9 us
    pallas_call x1, Pallas kernels, step(): pl.pallas_call(functools.partial(transport_kernel, elem_rows, levels), ou...  17.6 us
    ppermute x3, starting transfers between devices, shift_both(): lax.ppermute(backward_piece, axis, backward)  8 us
    transpose x2, local copies, waits for them, and re-layouts, step(): rows_first[:, :, -edge:].transpose(0, 2, 1)  5.58 us
    ppermute x3, waiting for transfers between devices, shift_both(): lax.ppermute(forward_piece, axis, forward)  4.72 us
    unnamed x17, local copies, waits for them, and re-layouts  4.29 us
    transpose x1, local copies, waits for them, and re-layouts, step(): jnp.pad(sides, ((0, 0), (0, node_cols - 2 * edge), (0, 0)))  4.08 us
  transfers between devices with their start and end apart: 6, of which 2 were waited for; matrix products, arithmetic and copies ran while one was open for 9% of the time, Pallas kernels for 53%

profile of v3, /device:TPU:0, one launch (start us, length us, event | category | flops | bytes accessed | tf_op | source)
XLA Modules:
  0.0 131.2 jit_solution(6169741722217273438)
XLA Ops:
  0.6 2.4 %copy.17 = f32[4,72,16,128]{3,1,0,2:T(8,128)S(1)} copy(f32[4,72,16,128]{3,2,1,0:T(8,128)} %param.10) | data formatting | bytes 4718592 | tf_op args[0]
  3.1 3.0 %slice_bitcast_fusion.1 = (f32[16,12,288]{1,2,0:T(8,128)}, f32[16,12,288]{1,2,0:T(8,128)}) fusion(f32[16,288,128]{2,1,0:T(8,128)S(1)} %bitcast.32), kind=kLoop, calls=%fused_computation.2 | loop fusion | bytes 884736 | tf_op jit(solution)/shard_map/transpose | solution.py:340
  6.1 2.6 %copy.19 = f32[16,12,288]{2,0,1:T(8,128)S(1)} copy(f32[16,12,288]{1,2,0:T(8,128)} %get-tuple-element.18) | data formatting | bytes 442368 | tf_op jit(solution)/shard_map/transpose | solution.py:340
  8.6 3.4 %collective-permute-start.1 = (f32[16,12,288]{2,0,1:T(8,128)S(1)}, f32[16,12,288]{2,0,1:T(8,128)S(1)}, u32[]{:S(2)}, u32[]{:S(2)}) collective-permute-start(f32[16,12,288]{2,0,1:T(8,128)S(1)} %copy.19), channel_id=1, source_target_pairs={{1,0},{2,1},{3,2},{4,3},{5,4},{6,5},{7,6},{0,7},{9,8},{10,9},{11,1... | collective-permute-start | bytes 663560 | tf_op jit(solution)/shard_map/ppermute | solution.py:272
  12.0 2.6 %copy.18 = f32[16,12,288]{2,0,1:T(8,128)S(1)} copy(f32[16,12,288]{1,2,0:T(8,128)} %get-tuple-element.17) | data formatting | bytes 442368 | tf_op jit(solution)/shard_map/transpose | solution.py:340
  14.6 0.1 collective-permute-start
  14.7 0.5 iota_add_fusion.1
  15.2 0.7 multiply_add_fusion
  15.9 1.3 %fusion.9 = (s32[4,32]{1,0:T(4,128)S(1)}, s32[4,32]{1,0:T(4,128)}) fusion(s32[32]{0:T(128)S(1)} %iota_add_fusion, s32[4,32]{1,0:T(4,128)} %param.14, s32[4]{0:T(128)} %iota_add_fusion.1), kind=kLoop, calls=%fused_computation.44 | loop fusion | flops 6272 | bytes 1680 | tf_op jit(solution)/shard_map/mul | solution.py:356
  17.3 0.7 broadcast_in_dim.7
  18.0 1.5 %reshape.356 = s32[4,128]{1,0:T(4,128)} reshape(s32[4,32,4]{2,1,0:T(8,128)} %broadcast_in_dim.7) | data formatting | bytes 4096 | tf_op jit(solution)/shard_map/reshape | solution.py:356
  19.5 1.4 %broadcast_in_dim.6 = s32[4,32,4]{2,1,0:T(8,128)} broadcast(s32[4,32]{1,0:T(4,128)} %get-tuple-element.34), dimensions={0,1} | broadcast | bytes 2560 | tf_op jit(solution)/shard_map/broadcast_in_dim | solution.py:357
  20.9 1.5 %mul.239 = s32[4,128]{1,0:T(4,128)} reshape(s32[4,32,4]{2,1,0:T(8,128)} %broadcast_in_dim.6) | data formatting | bytes 4096 | tf_op jit(solution)/shard_map/mul | solution.py:363
  22.4 0.7 fusion.11
  23.1 0.1 copy.21
  23.3 0.1 copy.20
  23.4 1.6 %collective-permute-start.2 = (f32[4,24,288]{2,1,0:T(8,128)S(1)}, f32[4,24,288]{2,1,0:T(8,128)S(1)}, u32[]{:S(2)}, u32[]{:S(2)}) collective-permute-start(f32[4,24,288]{2,1,0:T(8,128)S(1)} %get-tuple-element.19), channel_id=1, source_target_pairs={{0,8},{8,16},{16,24},{24,0},{1,9},{9,17},{17,25},{25,1},{2,10},{10... | collective-permute-start | bytes 331784 | tf_op jit(solution)/shard_map/ppermute | solution.py:272
  25.1 2.2 %collective-permute-start.3 = (f32[4,24,288]{2,1,0:T(8,128)S(1)}, f32[4,24,288]{2,1,0:T(8,128)S(1)}, u32[]{:S(2)}, u32[]{:S(2)}) collective-permute-start(f32[4,24,288]{2,1,0:T(8,128)S(1)} %get-tuple-element.20), channel_id=1, source_target_pairs={{8,0},{16,8},{24,16},{0,24},{9,1},{17,9},{25,17},{1,25},{10,2},{18... | collective-permute-start | bytes 331784 | tf_op jit(solution)/shard_map/ppermute | solution.py:272
  27.3 4.7 %collective-permute-done.2 = f32[4,24,288]{2,1,0:T(8,128)S(1)} collective-permute-done((f32[4,24,288]{2,1,0:T(8,128)S(1)}, f32[4,24,288]{2,1,0:T(8,128)S(1)}, u32[]{:S(2)}, u32[]{:S(2)}) %collective-permute-start.2) | collective-permute-done | bytes 110624 | tf_op jit(solution)/shard_map/ppermute | solution.py:272
  32.0 1.4 %collective-permute-done.3 = f32[4,24,288]{2,1,0:T(8,128)S(1)} collective-permute-done((f32[4,24,288]{2,1,0:T(8,128)S(1)}, f32[4,24,288]{2,1,0:T(8,128)S(1)}, u32[]{:S(2)}, u32[]{:S(2)}) %collective-permute-start.3) | collective-permute-done | bytes 110624 | tf_op jit(solution)/shard_map/ppermute | solution.py:272
  33.4 0.1 pad_maximum_fusion
  33.5 2.4 %copy.22 = f32[24,24,288]{1,2,0:T(8,128)} copy(f32[24,24,288]{2,1,0:T(8,128)S(1)} %pad_maximum_fusion) | data formatting | bytes 1327104 | tf_op jit(solution)/shard_map/concatenate | solution.py:344
  35.9 4.1 %pad_bitcast_fusion.halo = f32[24,288,128]{2,1,0:T(8,128)} fusion(f32[24,24,288]{1,2,0:T(8,128)} %copy.22), kind=kLoop, calls=%fused_computation | loop fusion | bytes 4202496 | tf_op jit(solution)/shard_map/transpose | solution.py:345
  40.0 0.0 copy-start.3
  40.0 0.1 fusion.19
  40.1 2.4 %collective-permute-start.5 = (f32[4,288,128]{2,1,0:T(8,128)S(1)}, f32[4,288,128]{2,1,0:T(8,128)S(1)}, u32[]{:S(2)}, u32[]{:S(2)}) collective-permute-start(f32[4,288,128]{2,1,0:T(8,128)S(1)} %get-tuple-element.15), channel_id=1, source_target_pairs={{8,0},{16,8},{24,16},{0,24},{9,1},{17,9},{25,17},{1,25},{10,2},{18... | collective-permute-start | bytes 1769480 | tf_op jit(solution)/shard_map/ppermute | solution.py:272
  42.5 0.1 broadcast_in_dim.16.rate
  42.7 68.9 %waves.1 = (f32[72,16,128]{2,1,0:T(8,128)S(1)}, f32[2,72,16,128]{3,2,1,0:T(8,128)S(1)}) custom-call(f32[72,16,128]{2,1,0:T(8,128)S(1)} %copy-done.1, f32[2,72,16,128]{3,2,1,0:T(8,128)S(1)} %copy-done, f32[72,1,128]{2,1,0:T(1,128)S(1)} %broadcast_in_dim.16.rate, f32[7,16,128]{2,1,0:T(8,128)S(1)} %copy-done.3, f32[7,16,128]{2,1,0:T(8,128)S(1)} %copy-done.2, ...), custom_call_target="tpu_custom_call" | custom-call | flops 300000000 | bytes 60000000 | tf_op jit(solution)/shard_map/waves/pallas_call | solution.py:230
  111.6 0.2 copy.25
  111.8 17.6 %transport.1 = f32[288,16,128]{2,1,0:T(8,128)} custom-call(f32[4,288,128]{2,1,0:T(8,128)S(1)} %collective-permute-done.4.low, f32[16,288,128]{2,1,0:T(8,128)S(1)} %bitcast.34, f32[4,288,128]{2,1,0:T(8,128)S(1)} %collective-permute-done.5.high, f32[24,288,128]{2,1,0:T(8,128)} %pad_bitcast_fusion.halo, s32[4,512]{1,0:T(4,128)S(1)} %pad_add_fusion.target, ...), custom_call_target="tpu_custom_call" | custom-call | tf_op jit(solution)/shard_map/transport/pallas_call | solution.py:366
  129.4 0.8 copy.28
  130.2 1.0 copy.29
  (24 shorter events, 0.1 us)
Async XLA Ops:
  8.6 14.5 %collective-permute-start.1 = (f32[16,12,288]{2,0,1:T(8,128)S(1)}, f32[16,12,288]{2,0,1:T(8,128)S(1)}, u32[]{:S(2)}, u32[]{:S(2)}) collective-permute-start(f32[16,12,288]{2,0,1:T(8,128)S(1)} %copy.19), channel_id=1, source_target_pairs={{1,0},{2,1},{3,2},{4,3},{5,4},{6,5},{7,6},{0,7},{9,8},{10,9},{11,1... | collective-permute-start | bytes 663560 | tf_op jit(solution)/shard_map/ppermute | solution.py:272
  14.6 8.6 %collective-permute-start = (f32[16,12,288]{2,0,1:T(8,128)S(1)}, f32[16,12,288]{2,0,1:T(8,128)S(1)}, u32[]{:S(2)}, u32[]{:S(2)}) collective-permute-start(f32[16,12,288]{2,0,1:T(8,128)S(1)} %copy.18), channel_id=1, source_target_pairs={{0,1},{1,2},{2,3},{3,4},{4,5},{5,6},{6,7},{7,0},{8,9},{9,10},{10,1... | collective-permute-start | bytes 663560 | tf_op jit(solution)/shard_map/ppermute | solution.py:272
  23.4 8.6 %collective-permute-start.2 = (f32[4,24,288]{2,1,0:T(8,128)S(1)}, f32[4,24,288]{2,1,0:T(8,128)S(1)}, u32[]{:S(2)}, u32[]{:S(2)}) collective-permute-start(f32[4,24,288]{2,1,0:T(8,128)S(1)} %get-tuple-element.19), channel_id=1, source_target_pairs={{0,8},{8,16},{16,24},{24,0},{1,9},{9,17},{17,25},{25,1},{2,10},{10... | collective-permute-start | bytes 331784 | tf_op jit(solution)/shard_map/ppermute | solution.py:272
  25.1 8.3 %collective-permute-start.3 = (f32[4,24,288]{2,1,0:T(8,128)S(1)}, f32[4,24,288]{2,1,0:T(8,128)S(1)}, u32[]{:S(2)}, u32[]{:S(2)}) collective-permute-start(f32[4,24,288]{2,1,0:T(8,128)S(1)} %get-tuple-element.20), channel_id=1, source_target_pairs={{8,0},{16,8},{24,16},{0,24},{9,1},{17,9},{25,17},{1,25},{10,2},{18... | collective-permute-start | bytes 331784 | tf_op jit(solution)/shard_map/ppermute | solution.py:272
  39.9 2.6 %copy-start.6 = (f32[72]{0:T(128)S(1)}, f32[72]{0:T(128)}, u32[]{:S(2)}) copy-start(f32[72]{0:T(128)} %param.13) | copy-start | bytes 868
  39.9 2.7 %copy-start = (f32[2,72,16,128]{3,2,1,0:T(8,128)S(1)}, f32[2,72,16,128]{3,2,1,0:T(8,128)}, u32[]{:S(2)}) copy-start(f32[2,72,16,128]{3,2,1,0:T(8,128)} %winds) | copy-start | bytes 3538948
  39.9 2.7 %copy-start.1 = (f32[72,16,128]{2,1,0:T(8,128)S(1)}, f32[72,16,128]{2,1,0:T(8,128)}, u32[]{:S(2)}) copy-start(f32[72,16,128]{2,1,0:T(8,128)} %thickness) | copy-start | bytes 1769476
  39.9 2.7 %copy-start.2 = (f32[7,16,128]{2,1,0:T(8,128)S(1)}, f32[7,16,128]{2,1,0:T(8,128)}, u32[]{:S(2)}) copy-start(f32[7,16,128]{2,1,0:T(8,128)} %constant.160.clone.by_row) | copy-start | bytes 172036
  40.0 2.7 %copy-start.3 = (f32[7,16,128]{2,1,0:T(8,128)S(1)}, f32[7,16,128]{2,1,0:T(8,128)}, u32[]{:S(2)}) copy-start(f32[7,16,128]{2,1,0:T(8,128)} %constant.159.clone.by_col) | copy-start | bytes 172036
  40.0 2.7 %copy-start.4 = (f32[2,16,128]{2,1,0:T(8,128)S(1)}, f32[2,16,128]{2,1,0:T(8,128)}, u32[]{:S(2)}) copy-start(f32[2,16,128]{2,1,0:T(8,128)} %constant.162.clone.put) | copy-start | bytes 49156
  40.0 2.7 %copy-start.5 = (f32[2,8,128]{2,1,0:T(8,128)S(1)}, f32[2,8,128]{2,1,0:T(8,128)}, u32[]{:S(2)}) copy-start(f32[2,8,128]{2,1,0:T(8,128)} %constant.161.clone.take) | copy-start | bytes 24580
  40.1 71.7 %collective-permute-start.5 = (f32[4,288,128]{2,1,0:T(8,128)S(1)}, f32[4,288,128]{2,1,0:T(8,128)S(1)}, u32[]{:S(2)}, u32[]{:S(2)}) collective-permute-start(f32[4,288,128]{2,1,0:T(8,128)S(1)} %get-tuple-element.15), channel_id=1, source_target_pairs={{8,0},{16,8},{24,16},{0,24},{9,1},{17,9},{25,17},{1,25},{10,2},{18... | collective-permute-start | bytes 1769480 | tf_op jit(solution)/shard_map/ppermute | solution.py:272
  42.4 69.4 %collective-permute-start.4 = (f32[4,288,128]{2,1,0:T(8,128)S(1)}, f32[4,288,128]{2,1,0:T(8,128)S(1)}, u32[]{:S(2)}, u32[]{:S(2)}) collective-permute-start(f32[4,288,128]{2,1,0:T(8,128)S(1)} %get-tuple-element.16), channel_id=1, source_target_pairs={{0,8},{8,16},{16,24},{24,0},{1,9},{9,17},{17,25},{25,1},{2,10},{10... | collective-permute-start | bytes 1769480 | tf_op jit(solution)/shard_map/ppermute | solution.py:272
